TPU v7x, 32 devices: a whole 2x2x4 slice. The times are simulated.
32 devices in a mesh: shore: 4 (over x, core), cross: 8 (over z, y).
Axes of the slice: x: 2, y: 2, z: 4, core: 2. Of those that a mesh axis runs over, the one named last changes fastest.
Arguments:
- positions: float32 [2, 64, 64, 128], P(None, 'shore', 'cross'), may hold values from 0 to 1
- velocity: float32 [2, 64, 64, 128], P(None, 'shore', 'cross'), may hold values from -3 to 3
- density: float32 [64, 64, 128], P('shore', 'cross'), may hold values from 0.97 to 1.03
- particle_mass: float32 [64, 64, 128], P('shore', 'cross'), may hold values from 0.004 to 0.016
- cell_count: int32 [64, 64], P('shore', 'cross'), may hold values from 0 to 128
- wind_seed: int32 [64, 64, 128], P('shore', 'cross'), may hold values from 0 to 15
- wind_table: float32 [2, 16], replicated, may hold values from -4 to 4
- migrant_slot: int32 [4, 8, 4, 1792], P('shore', 'cross'), may hold values from 0 to 16383
- migrant_count: int32 [4, 8, 4], P('shore', 'cross'), may hold values from 896 to 1792, as said below
Outputs:
- state_next: float32 [7, 64, 64, 128], P(None, 'shore', 'cross')
- arrivals: float32 [4, 8, 4, 8, 1792], P('shore', 'cross')
Inputs may be any that keep to these rules, and one draw needn't show every extreme that they name: `migrant_slot`: a slot in one device's own blocks, numbered (block along * 8 + block across) * 128 + slot. `migrant_count`: on every device, at least one direction has exactly 1792 migrants.
All inputs are finite; a program needn't handle non-finite values.
Results may differ from a plain program's by a relative error of at most 0.0003.
Values sent between devices are 32-bit elements; how exact they have to be, the bound alone decides.
No kernel may reach another device: no remote copies, remote signals or barrier semaphores. Data moves between devices by JAX's collectives and lax.ppermute only.
A program may use at most 64 MiB of HBM per device.

v0:
```python
import jax
import jax.numpy as jnp
from jax import lax
from jax.sharding import PartitionSpec as P

sound_speed = 10.0
smooth = 0.5
viscous = 0.1
kernel_norm = 7.0 / (4.0 * 3.141592653589793 * smooth * smooth)
grad_coef = -5.0 * kernel_norm / (smooth * smooth)


def passed_along(array, axis, by):
    peers = lax.axis_size(axis)
    pairs = [(i, i + by) for i in range(peers) if 0 <= i + by < peers]
    return lax.ppermute(array, axis, pairs)


def padded(cells, sides, width):
    for axis, dim in sides:
        count = lax.axis_size(axis)
        ends = count - 1
        head = lax.slice_in_dim(cells, 0, width, axis=dim)
        tail = lax.slice_in_dim(cells, cells.shape[dim] - width, cells.shape[dim], axis=dim)
        cells = jnp.concatenate(
            [
                lax.ppermute(tail, axis, [(i, (i + 1) % count) for i in range(ends)]),
                cells,
                lax.ppermute(head, axis, [((i + 1) % count, i) for i in range(ends)]),
            ],
            axis=dim,
        )
    return cells


def pressure_ratio(density):
    cube = density * density * density
    seventh = cube * cube * density
    pressure = sound_speed * sound_speed / 7.0 * (seventh - 1.0)
    return pressure / (density * density)


def pack_fields(positions, velocity, density, particle_mass, live_slots):
    return jnp.stack(
        [
            positions[0],
            positions[1],
            velocity[0],
            velocity[1],
            density,
            particle_mass,
            live_slots,
            pressure_ratio(density),
        ]
    )


def tile_terms(own_cells, near_cells, step_x, step_y):
    offset_x = own_cells[0][:, :, None] - near_cells[0][:, None, :] - step_x
    offset_y = own_cells[1][:, :, None] - near_cells[1][:, None, :] - step_y
    dist_sq = offset_x * offset_x + offset_y * offset_y
    radius = jnp.sqrt(dist_sq) / smooth
    falloff = jnp.maximum(1.0 - 0.5 * radius, 0.0)
    gradient = grad_coef * falloff * falloff * falloff
    relative_u = own_cells[2][:, :, None] - near_cells[2][:, None, :]
    relative_v = own_cells[3][:, :, None] - near_cells[3][:, None, :]
    approach = relative_u * offset_x + relative_v * offset_y
    viscous_mu = smooth * jnp.minimum(approach, 0.0) / (dist_sq + 0.01 * smooth * smooth)
    mean_density = 0.5 * (own_cells[4][:, :, None] + near_cells[4][:, None, :])
    visc_term = -viscous * sound_speed * viscous_mu / mean_density
    weighted = (near_cells[5] * near_cells[6])[:, None, :] * gradient
    coupling = weighted * (own_cells[7][:, :, None] + near_cells[7][:, None, :] + visc_term)
    force_x = -jnp.sum(coupling * offset_x, axis=2)
    force_y = -jnp.sum(coupling * offset_y, axis=2)
    density_rate = jnp.sum(weighted * approach, axis=2)
    return jnp.stack([force_x, force_y, density_rate])


def tile_both(own_cells, near_cells, step_x, step_y):
    offset_x = own_cells[0][:, :, None] - near_cells[0][:, None, :] - step_x
    offset_y = own_cells[1][:, :, None] - near_cells[1][:, None, :] - step_y
    dist_sq = offset_x * offset_x + offset_y * offset_y
    radius = jnp.sqrt(dist_sq) / smooth
    falloff = jnp.maximum(1.0 - 0.5 * radius, 0.0)
    gradient = grad_coef * falloff * falloff * falloff
    relative_u = own_cells[2][:, :, None] - near_cells[2][:, None, :]
    relative_v = own_cells[3][:, :, None] - near_cells[3][:, None, :]
    approach = relative_u * offset_x + relative_v * offset_y
    viscous_mu = smooth * jnp.minimum(approach, 0.0) / (dist_sq + 0.01 * smooth * smooth)
    mean_density = 0.5 * (own_cells[4][:, :, None] + near_cells[4][:, None, :])
    visc_term = -viscous * sound_speed * viscous_mu / mean_density
    shared = gradient * (own_cells[7][:, :, None] + near_cells[7][:, None, :] + visc_term)
    shared_x = shared * offset_x
    shared_y = shared * offset_y
    rate_part = gradient * approach
    near_mass = (near_cells[5] * near_cells[6])[:, None, :]
    own_mass = (own_cells[5] * own_cells[6])[:, :, None]
    front = jnp.stack(
        [
            -jnp.sum(near_mass * shared_x, axis=2),
            -jnp.sum(near_mass * shared_y, axis=2),
            jnp.sum(near_mass * rate_part, axis=2),
        ]
    )
    behind = jnp.stack(
        [
            jnp.sum(own_mass * shared_x, axis=1),
            jnp.sum(own_mass * shared_y, axis=1),
            jnp.sum(own_mass * rate_part, axis=1),
        ]
    )
    return (front, behind)


def half_row(three_rows):
    own_cells = three_rows[:, 1, 1:-1]
    width = own_cells.shape[1]
    own_sum = tile_terms(own_cells, own_cells, 0.0, 0.0)
    front, behind = tile_both(own_cells, three_rows[:, 1, 2 : 2 + width], 0.0, 1.0)
    own_sum = own_sum + front
    row_here = jnp.pad(behind, ((0, 0), (2, 0), (0, 0)))
    row_next = jnp.zeros_like(row_here)
    for step_y in (-1, 0, 1):
        near_cells = three_rows[:, 2, 1 + step_y : 1 + step_y + width]
        front, behind = tile_both(own_cells, near_cells, 1.0, float(step_y))
        own_sum = own_sum + front
        row_next = row_next + jnp.pad(behind, ((0, 0), (1 + step_y, 1 - step_y), (0, 0)))
    row_here = row_here + jnp.pad(own_sum, ((0, 0), (1, 1), (0, 0)))
    return (row_here, row_next)


def across_return(block, offset):
    return passed_along(block, "cross", offset)


def half_forces(extended):
    row_count = extended.shape[1] - 2
    col_count = extended.shape[2] - 2

    def one_row(row_index):
        return half_row(lax.dynamic_slice_in_dim(extended, row_index, 3, 1))

    here_rows, next_rows = lax.map(one_row, jnp.arange(row_count, dtype=jnp.int32))
    here_rows = jnp.transpose(here_rows, (1, 0, 2, 3))
    next_rows = jnp.transpose(next_rows, (1, 0, 2, 3))
    total = jnp.pad(here_rows, ((0, 0), (1, 1), (0, 0), (0, 0))) + jnp.pad(
        next_rows, ((0, 0), (2, 0), (0, 0), (0, 0))
    )
    arrived = passed_along(total[:, row_count + 1], "shore", 1)
    total = total.at[:, 1].add(arrived)
    upper = across_return(total[:, 1 : row_count + 1, col_count + 1], 1)
    lower = across_return(total[:, 1 : row_count + 1, 0], -1)
    total = total.at[:, 1 : row_count + 1, 1].add(upper)
    total = total.at[:, 1 : row_count + 1, col_count].add(lower)
    return total[:, 1 : row_count + 1, 1 : col_count + 1]


def time_step(peak_acc, peak_speed):
    return 0.25 * smooth / (sound_speed + peak_speed + jnp.sqrt(smooth * peak_acc))


def pick_migrants(flattened, slot_list, live_count):
    width = slot_list.shape[1]
    picked = jnp.take(flattened, slot_list.reshape(-1), axis=1)
    picked = jnp.transpose(picked.reshape(flattened.shape[0], 4, width), (1, 0, 2))
    live_rows = (jnp.arange(width, dtype=jnp.int32)[None, :] < live_count[:, None]).astype(
        jnp.float32
    )
    return picked * live_rows[:, None, :]


def along_shore(block, offset):
    return passed_along(block, "shore", offset)


def across_shore(block, offset):
    return passed_along(block, "cross", offset)


def body(
    positions,
    velocity,
    density,
    particle_mass,
    cell_count,
    wind_seed,
    wind_table,
    migrant_slot,
    migrant_count,
):
    slot_total = positions.shape[3]
    slot_ids = jnp.arange(slot_total, dtype=jnp.int32)
    live_slots = (slot_ids[None, None, :] < cell_count[:, :, None]).astype(jnp.float32)
    fields = pack_fields(positions, velocity, density, particle_mass, live_slots)
    extended = padded(fields, (("shore", 1), ("cross", 2)), 1)
    forces = half_forces(extended)
    level_ids = jnp.arange(wind_table.shape[1], dtype=jnp.int32)
    one_hot = (wind_seed[None] == level_ids[:, None, None, None]).astype(jnp.float32)
    windage = jnp.einsum("cl,lxyp->cxyp", wind_table, one_hot, precision=lax.Precision.HIGHEST)
    acceleration = (forces[:2] + windage) * live_slots[None]
    density_rate = forces[2] * live_slots
    local_acc = jnp.max(
        jnp.sqrt(acceleration[0] * acceleration[0] + acceleration[1] * acceleration[1])
    )
    local_speed = jnp.max(
        jnp.sqrt(velocity[0] * velocity[0] + velocity[1] * velocity[1]) * live_slots
    )
    peak_acc, peak_speed = lax.pmax((local_acc, local_speed), ("shore", "cross"))
    delta_t = time_step(peak_acc, peak_speed)
    new_velocity = (velocity + delta_t * acceleration) * live_slots[None]
    new_position = (positions + delta_t * new_velocity) * live_slots[None]
    new_density = (density + delta_t * density_rate) * live_slots
    state_next = jnp.concatenate([new_position, new_velocity, new_density[None], acceleration])
    carried = jnp.concatenate(
        [
            new_position,
            new_velocity,
            new_density[None],
            (particle_mass * live_slots)[None],
            acceleration,
        ]
    )
    flattened = carried.reshape(carried.shape[0], -1)
    leaving = pick_migrants(flattened, migrant_slot[0, 0], migrant_count[0, 0])
    eastward = along_shore(leaving[0], 1)
    westward = along_shore(leaving[1], -1)
    northward = across_shore(leaving[2], 1)
    southward = across_shore(leaving[3], -1)
    arrivals = jnp.stack([eastward, westward, northward, southward])[None, None]
    return (state_next, arrivals)


def solution(mesh):
    in_specs = (
        P(None, "shore", "cross", None),
        P(None, "shore", "cross", None),
        P("shore", "cross", None),
        P("shore", "cross", None),
        P("shore", "cross"),
        P("shore", "cross", None),
        P(),
        P("shore", "cross", None, None),
        P("shore", "cross", None),
    )
    out_specs = (P(None, "shore", "cross", None), P("shore", "cross", None, None, None))
    return jax.shard_map(body, mesh=mesh, in_specs=in_specs, out_specs=out_specs, check_vma=False)
```

profile of v0, /device:TPU:6, one launch (start us, length us, event | category | flops | bytes accessed | tf_op | source)
XLA Modules:
  0.0 304.9 jit_solution(5961585366200237696)
XLA Ops:
  7.9 3.6 %collective-permute-start.1 = (f32[8,1,8,128]{3,2,1,0:T(8,128)S(1)}, f32[8,1,8,128]{3,2,1,0:T(8,128)S(1)}, u32[]{:S(2)}, u32[]{:S(2)}) collective-permute-start(f32[8,1,8,128]{3,2,1,0:T(8,128)S(1)} %get-tuple-element.237), channel_id=1, source_target_pairs={{8,0},{16,8},{24,16},{9,1},{17,9},{25,17},{10,2},{18,10},{26,18},{... | collective-permute-start | bytes 98312 | tf_op jit(solution)/shard_map/ppermute | solution.py:29
  13.2 3.4 %collective-permute-start.2 = (f32[8,18,1,128]{3,2,1,0:T(1,128)S(1)}, f32[8,18,1,128]{3,2,1,0:T(1,128)S(1)}, u32[]{:S(2)}, u32[]{:S(2)}) collective-permute-start(f32[8,18,1,128]{3,2,1,0:T(1,128)S(1)} %get-tuple-element.234), channel_id=1, source_target_pairs={{0,1},{1,2},{2,3},{3,4},{4,5},{5,6},{6,7},{8,9},{9,10},{10,11},{11... | collective-permute-start | bytes 221192 | tf_op jit(solution)/shard_map/ppermute | solution.py:27
  19.5 4.3 %collective-permute-done.3 = f32[8,18,1,128]{3,2,1,0:T(1,128)S(1)} collective-permute-done((f32[8,18,1,128]{3,2,1,0:T(1,128)S(1)}, f32[8,18,1,128]{3,2,1,0:T(1,128)S(1)}, u32[]{:S(2)}, u32[]{:S(2)}) %collective-permute-start.3) | collective-permute-done | bytes 73760 | tf_op jit(solution)/shard_map/ppermute | solution.py:29
  24.0 170.1 %while.18 = (s32[]{:T(128)}, f32[16,3,10,128]{3,1,2,0:T(4,128)S(1)}, f32[16,3,10,128]{3,1,2,0:T(4,128)S(1)}, s32[16]{0:T(128)S(1)}, f32[8,18,10,128]{3,2,1,0:T(8...) while((s32[]{:T(128)}, ...), condition=%wide.region_30.31_spmd, body=%wide.region_2.30_spmd.sunk | while | flops 26749708 | bytes 985423 | solution.py:143
  26.7 2.6 multiply_reduce_fusion.32
  37.3 2.6 multiply_reduce_fusion.32
  48.0 2.6 multiply_reduce_fusion.32
  58.6 2.6 multiply_reduce_fusion.32
  69.2 2.6 multiply_reduce_fusion.32
  79.9 2.6 multiply_reduce_fusion.32
  90.5 2.6 multiply_reduce_fusion.32
  111.8 2.6 multiply_reduce_fusion.32
  143.7 2.6 multiply_reduce_fusion.32
  175.6 2.6 multiply_reduce_fusion.32
  196.4 3.0 collective-permute-done.4
  202.8 3.3 %collective-permute-start.6 = (f32[3,16,128]{2,1,0:T(8,128)S(1)}, f32[3,16,128]{2,1,0:T(8,128)S(1)}, u32[]{:S(2)}, u32[]{:S(2)}) collective-permute-start(f32[3,16,128]{2,1,0:T(8,128)S(1)} %get-tuple-element.238), channel_id=1, source_target_pairs={{1,0},{2,1},{3,2},{4,3},{5,4},{6,5},{7,6},{9,8},{10,9},{11,10},{12... | collective-permute-start | bytes 73736 | tf_op jit(solution)/shard_map/ppermute | solution.py:16
  206.5 2.9 collective-permute-done.6
  210.2 40.7 %all-reduce.7 = (f32[]{:T(128)}, f32[]{:T(128)}) all-reduce(f32[]{:T(128)} %fusion.93, f32[]{:T(128)} %fusion.92), channel_id=1, replica_groups=mesh['shore'=4,'cross'=8] {'shore','cross'}, use_global_device_ids=true, to_apply=%region_1.0 | all-reduce | flops 2 | bytes 16 | tf_op jit(solution)/shard_map/pmax | solution.py:208
  253.4 5.3 %copy.81 = f32[8,16384]{0,1:T(8,128)} copy(f32[8,16384]{1,0:T(8,128)S(1)} %concatenate.38) | data formatting | bytes 1048576 | tf_op jit(solution)/shard_map/concatenate | solution.py:214
  258.7 27.5 %gather_fusion = f32[7168,8]{1,0:T(8,128)} fusion(f32[8,16384]{0,1:T(8,128)} %copy.81, s32[7168]{0:T(1024)S(1)} %broadcast_clamp_fusion), kind=kCustom, calls=%fused_computation | custom fusion | bytes 487424 | tf_op jit(solution)/shard_map/jit(_take)/gather | solution.py:164
  290.7 3.6 %collective-permute-start.8 = (f32[8,1792]{1,0:T(8,128)S(1)}, f32[8,1792]{1,0:T(8,128)S(1)}, u32[]{:S(2)}, u32[]{:S(2)}) collective-permute-start(f32[8,1792]{1,0:T(8,128)S(1)} %get-tuple-element.243), channel_id=1, source_target_pairs={{8,0},{16,8},{24,16},{9,1},{17,9},{25,17},{10,2},{18,10},{26,18},{... | collective-permute-start | bytes 172040 | tf_op jit(solution)/shard_map/ppermute | solution.py:16
  294.4 2.9 collective-permute-start.9
  297.3 3.0 collective-permute-start.10
  301.1 3.2 %collective-permute-done.10 = f32[8,1792]{1,0:T(8,128)S(1)} collective-permute-done((f32[8,1792]{1,0:T(8,128)S(1)}, f32[8,1792]{1,0:T(8,128)S(1)}, u32[]{:S(2)}, u32[]{:S(2)}) %collective-permute-start.10) | collective-permute-done | bytes 57376 | tf_op jit(solution)/shard_map/ppermute | solution.py:16
  (382 shorter events, 136.6 us)
Async XLA Ops:
  0.6 11.8 %copy-start = (f32[2,16]{1,0:T(2,128)S(1)}, f32[2,16]{1,0:T(2,128)}, u32[]{:S(2)}) copy-start(f32[2,16]{1,0:T(2,128)} %param.23) | copy-start | bytes 388
  0.6 11.7 %copy-start.5 = (s32[1,1,4,1792]{3,2,1,0:T(4,128)S(1)}, s32[1,1,4,1792]{3,2,1,0:T(4,128)}, u32[]{:S(2)}) copy-start(s32[1,1,4,1792]{3,2,1,0:T(4,128)} %param.24) | copy-start | bytes 86020
  0.7 11.7 %copy-start.6 = (s32[1,1,4]{2,1,0:T(1,128)S(1)}, s32[1,1,4]{2,1,0:T(1,128)}, u32[]{:S(2)}) copy-start(s32[1,1,4]{2,1,0:T(1,128)} %param.25) | copy-start | bytes 52
  0.7 11.8 %copy-start.7 = (s32[16,8,128]{2,1,0:T(8,128)S(1)}, s32[16,8,128]{2,1,0:T(8,128)}, u32[]{:S(2)}) copy-start(s32[16,8,128]{2,1,0:T(8,128)} %param.22) | copy-start | bytes 196612
  6.0 6.9 %collective-permute-start = (f32[8,1,8,128]{3,2,1,0:T(8,128)S(1)}, f32[8,1,8,128]{3,2,1,0:T(8,128)S(1)}, u32[]{:S(2)}, u32[]{:S(2)}) collective-permute-start(f32[8,1,8,128]{3,2,1,0:T(8,128)S(1)} %get-tuple-element.236), channel_id=1, source_target_pairs={{0,8},{8,16},{16,24},{1,9},{9,17},{17,25},{2,10},{10,18},{18,26},{... | collective-permute-start | bytes 98312 | tf_op jit(solution)/shard_map/ppermute | solution.py:27
  7.9 5.2 %collective-permute-start.1 = (f32[8,1,8,128]{3,2,1,0:T(8,128)S(1)}, f32[8,1,8,128]{3,2,1,0:T(8,128)S(1)}, u32[]{:S(2)}, u32[]{:S(2)}) collective-permute-start(f32[8,1,8,128]{3,2,1,0:T(8,128)S(1)} %get-tuple-element.237), channel_id=1, source_target_pairs={{8,0},{16,8},{24,16},{9,1},{17,9},{25,17},{10,2},{18,10},{26,18},{... | collective-permute-start | bytes 98312 | tf_op jit(solution)/shard_map/ppermute | solution.py:29
  13.2 6.2 %collective-permute-start.2 = (f32[8,18,1,128]{3,2,1,0:T(1,128)S(1)}, f32[8,18,1,128]{3,2,1,0:T(1,128)S(1)}, u32[]{:S(2)}, u32[]{:S(2)}) collective-permute-start(f32[8,18,1,128]{3,2,1,0:T(1,128)S(1)} %get-tuple-element.234), channel_id=1, source_target_pairs={{0,1},{1,2},{2,3},{3,4},{4,5},{5,6},{6,7},{8,9},{9,10},{10,11},{11... | collective-permute-start | bytes 221192 | tf_op jit(solution)/shard_map/ppermute | solution.py:27
  16.7 7.1 %collective-permute-start.3 = (f32[8,18,1,128]{3,2,1,0:T(1,128)S(1)}, f32[8,18,1,128]{3,2,1,0:T(1,128)S(1)}, u32[]{:S(2)}, u32[]{:S(2)}) collective-permute-start(f32[8,18,1,128]{3,2,1,0:T(1,128)S(1)} %get-tuple-element.235), channel_id=1, source_target_pairs={{1,0},{2,1},{3,2},{4,3},{5,4},{6,5},{7,6},{9,8},{10,9},{11,10},{12... | collective-permute-start | bytes 221192 | tf_op jit(solution)/shard_map/ppermute | solution.py:29
  194.1 7.9 %copy-start.1 = (f32[2,16,8,128]{3,2,1,0:T(8,128)S(1)}, f32[2,16,8,128]{3,2,1,0:T(8,128)}, u32[]{:S(2)}) copy-start(f32[2,16,8,128]{3,2,1,0:T(8,128)} %param.18) | copy-start | bytes 393220
  194.2 5.2 %collective-permute-start.4 = (f32[3,10,128]{2,0,1:T(4,128)S(1)}, f32[3,10,128]{2,0,1:T(4,128)S(1)}, u32[]{:S(2)}, u32[]{:S(2)}) collective-permute-start(f32[3,10,128]{2,0,1:T(4,128)S(1)} %get-tuple-element.232), channel_id=1, source_target_pairs={{0,8},{8,16},{16,24},{1,9},{9,17},{17,25},{2,10},{10,18},{18,26},{... | collective-permute-start | bytes 46088 | tf_op jit(solution)/shard_map/ppermute | solution.py:16
  196.4 55.9 %copy-start.3 = (f32[2,16,8,128]{3,2,1,0:T(8,128)S(1)}, f32[2,16,8,128]{3,2,1,0:T(8,128)}, u32[]{:S(2)}) copy-start(f32[2,16,8,128]{3,2,1,0:T(8,128)} %param.17) | copy-start | bytes 393220
  199.5 6.5 %collective-permute-start.5 = (f32[3,16,128]{2,1,0:T(8,128)S(1)}, f32[3,16,128]{2,1,0:T(8,128)S(1)}, u32[]{:S(2)}, u32[]{:S(2)}) collective-permute-start(f32[3,16,128]{2,1,0:T(8,128)S(1)} %get-tuple-element.239), channel_id=1, source_target_pairs={{0,1},{1,2},{2,3},{3,4},{4,5},{5,6},{6,7},{8,9},{9,10},{10,11},{11... | collective-permute-start | bytes 73736 | tf_op jit(solution)/shard_map/ppermute | solution.py:16
  202.8 6.6 %collective-permute-start.6 = (f32[3,16,128]{2,1,0:T(8,128)S(1)}, f32[3,16,128]{2,1,0:T(8,128)S(1)}, u32[]{:S(2)}, u32[]{:S(2)}) collective-permute-start(f32[3,16,128]{2,1,0:T(8,128)S(1)} %get-tuple-element.238), channel_id=1, source_target_pairs={{1,0},{2,1},{3,2},{4,3},{5,4},{6,5},{7,6},{9,8},{10,9},{11,10},{12... | collective-permute-start | bytes 73736 | tf_op jit(solution)/shard_map/ppermute | solution.py:16
  206.4 46.0 %copy-start.2 = (f32[16,8,128]{2,1,0:T(8,128)S(1)}, f32[16,8,128]{2,1,0:T(8,128)}, u32[]{:S(2)}) copy-start(f32[16,8,128]{2,1,0:T(8,128)} %param.19) | copy-start | bytes 196612
  206.4 46.0 %copy-start.4 = (f32[16,8,128]{2,1,0:T(8,128)S(1)}, f32[16,8,128]{2,1,0:T(8,128)}, u32[]{:S(2)}) copy-start(f32[16,8,128]{2,1,0:T(8,128)} %param.20) | copy-start | bytes 196612
  288.8 12.2 %collective-permute-start.7 = (f32[8,1792]{1,0:T(8,128)S(1)}, f32[8,1792]{1,0:T(8,128)S(1)}, u32[]{:S(2)}, u32[]{:S(2)}) collective-permute-start(f32[8,1792]{1,0:T(8,128)S(1)} %get-tuple-element.240), channel_id=1, source_target_pairs={{0,8},{8,16},{16,24},{1,9},{9,17},{17,25},{2,10},{10,18},{18,26},{... | collective-permute-start | bytes 172040 | tf_op jit(solution)/shard_map/ppermute | solution.py:16
  290.7 10.3 %collective-permute-start.8 = (f32[8,1792]{1,0:T(8,128)S(1)}, f32[8,1792]{1,0:T(8,128)S(1)}, u32[]{:S(2)}, u32[]{:S(2)}) collective-permute-start(f32[8,1792]{1,0:T(8,128)S(1)} %get-tuple-element.243), channel_id=1, source_target_pairs={{8,0},{16,8},{24,16},{9,1},{17,9},{25,17},{10,2},{18,10},{26,18},{... | collective-permute-start | bytes 172040 | tf_op jit(solution)/shard_map/ppermute | solution.py:16
  294.4 6.7 %collective-permute-start.9 = (f32[8,1792]{1,0:T(8,128)S(1)}, f32[8,1792]{1,0:T(8,128)S(1)}, u32[]{:S(2)}, u32[]{:S(2)}) collective-permute-start(f32[8,1792]{1,0:T(8,128)S(1)} %get-tuple-element.242), channel_id=1, source_target_pairs={{0,1},{1,2},{2,3},{3,4},{4,5},{5,6},{6,7},{8,9},{9,10},{10,11},{11... | collective-permute-start | bytes 172040 | tf_op jit(solution)/shard_map/ppermute | solution.py:16
  297.3 7.0 %collective-permute-start.10 = (f32[8,1792]{1,0:T(8,128)S(1)}, f32[8,1792]{1,0:T(8,128)S(1)}, u32[]{:S(2)}, u32[]{:S(2)}) collective-permute-start(f32[8,1792]{1,0:T(8,128)S(1)} %get-tuple-element.241), channel_id=1, source_target_pairs={{1,0},{2,1},{3,2},{4,3},{5,4},{6,5},{7,6},{9,8},{10,9},{11,10},{12... | collective-permute-start | bytes 172040 | tf_op jit(solution)/shard_map/ppermute | solution.py:16
where the time goes:
time: 306 us; the launch traced here: 305 us
  other arithmetic  131 us (43%)
  local copies, waits for them, and re-layouts  51.9 us (17%)
  blocking collectives  40.7 us (13%)
  loops' own time  33.5 us (11%)
  starting transfers between devices  30.7 us (10%)
  waiting for transfers between devices  13.9 us (5%)
    reduce_sum x48, other arithmetic, tile_both(): jnp.sum(own_mass * shared_x, axis=1)  82.4 us
    reduce_sum x16, other arithmetic, tile_both(): jnp.sum(near_mass * shared_x, axis=2)  40.8 us
    pmax x1, blocking collectives, body(): lax.pmax((local_acc, local_speed), ('shore', 'cross'))  40.7 us
    another operation x1, loops' own time, half_forces(): lax.map(one_row, jnp.arange(row_count, dtype=jnp.int32))  33.5 us
    gather x2, local copies, waits for them, and re-layouts, pick_migrants(): picked = jnp.take(flattened, slot_list.reshape(-1), axis=1)  30.1 us
    ppermute x7, starting transfers between devices, passed_along(): return lax.ppermute(array, axis, pairs)  19.3 us
    dynamic_slice x16, local copies, waits for them, and re-layouts, half_forces(): lax.map(one_row, jnp.arange(row_count, dtype=jnp.int32))  9.38 us
    ppermute x7, waiting for transfers between devices, passed_along(): return lax.ppermute(array, axis, pairs)  9.08 us
  transfers between devices with their start and end apart: 11, of which 6 were waited for; matrix products, arithmetic and copies ran while one was open for 1% of the time, Pallas kernels for 0%

commit v1 on v0

v1 whole, which is shorter than its diff:
```python
import functools

import jax
import jax.numpy as jnp
import numpy as np
from jax import lax
from jax.experimental import pallas as pl
from jax.experimental.pallas import tpu as pltpu
from jax.sharding import PartitionSpec as P

sound_speed = 10.0
smooth = 0.5
kernel_norm = 7.0 / (4.0 * 3.141592653589793 * smooth * smooth)
grad_coef = -5.0 * kernel_norm / (smooth * smooth)
f32 = jnp.float32
SUB = 8
GRAN = 2
VMEM_LIMIT = 48 * 1024 * 1024


def passed_along(array, axis, by):
    peers = lax.axis_size(axis)
    pairs = [(i, i + by) for i in range(peers) if 0 <= i + by < peers]
    return lax.ppermute(array, axis, pairs)


def everywhere_max(array):
    for axis in ("cross", "shore"):
        peers = lax.axis_size(axis)
        step = 1
        while step < peers:
            if peers & (peers - 1) == 0:
                pairs = [(i, i ^ step) for i in range(peers)]
            else:
                pairs = [(i, (i + step) % peers) for i in range(peers)]
            array = jnp.maximum(array, lax.ppermute(array, axis, pairs))
            step *= 2
    return array


def pressure_ratio(density):
    cube = density * density * density
    seventh = cube * cube * density
    pressure = sound_speed * sound_speed / 7.0 * (seventh - 1.0)
    return pressure / (density * density)


def pair_terms(own, near):
    dx = own[0] - near[0]
    dy = own[1] - near[1]
    dist_sq = dx * dx + dy * dy
    guarded = jnp.maximum(dist_sq, 1e-30)
    radius = guarded * lax.rsqrt(guarded)
    falloff = jnp.maximum(1.0 - radius, 0.0)
    weight = (falloff * falloff) * (falloff * (own[6] * near[6]))
    approach = (own[2] - near[2]) * dx + (own[3] - near[3]) * dy
    bottom = (dist_sq + 0.01 * smooth * smooth) * (own[4] + near[4])
    total = (own[5] + near[5]) - jnp.minimum(approach, 0.0) * pltpu.reciprocal(bottom, approx=True)
    shared = weight * total
    return shared * dx, shared * dy, weight * approach


def plus(total, term):
    return term if total is None else tuple(a + b for a, b in zip(total, term))


def center_tiles(q_ref, behind_ref, acc_ref, rows_ref, center, tiles, near):
    columns = jnp.transpose(q_ref[center])
    lanes = columns.shape[0]
    others = []
    for block, step_x, step_y, _ in near:
        fields = [q_ref[block, k : k + 1, :] for k in range(7)]
        fields[0] = fields[0] + step_x
        fields[1] = fields[1] + step_y
        others.append([jnp.broadcast_to(f, (SUB, lanes)) for f in fields])
    sums = [None] * len(near)
    both = any(two for _, _, _, two in near)
    for t in range(tiles):
        tile = columns[SUB * t : SUB * t + SUB]
        mine = [jnp.broadcast_to(tile[:, k : k + 1], (SUB, lanes)) for k in range(7)]
        behind = None
        for n in range(len(near)):
            term = pair_terms(others[n], mine)
            sums[n] = plus(sums[n], term)
            if near[n][3]:
                behind = plus(behind, term)
        if both:
            for k in range(3):
                behind_ref[k, SUB * t : SUB * t + SUB, :] = behind[k]
    for n in range(len(near)):
        for k in range(3):
            acc_ref[near[n][0], k] = acc_ref[near[n][0], k] + sums[n][k]
    if both:
        ones = jnp.ones((16, lanes), jnp.bfloat16)
        dims = (((1,), (1,)), ((), ()))
        sub = lax.broadcasted_iota(jnp.int32, (SUB, lanes), 0)
        total = jnp.zeros((SUB, lanes), f32)
        for k in range(3):
            part = behind_ref[k]
            high = part.astype(jnp.bfloat16)
            rest = part - high.astype(f32)
            mid = rest.astype(jnp.bfloat16)
            low = (rest - mid.astype(f32)).astype(jnp.bfloat16)
            row = sum(
                lax.dot_general(ones, piece, dims, preferred_element_type=f32)
                for piece in (high, mid, low)
            )
            total = jnp.where(sub == k, row[:SUB], total)
        rows_ref[center] = total


def center_block(q_ref, behind_ref, acc_ref, rows_ref, center, count, near):
    most = q_ref.shape[2] // SUB
    tiles = pl.cdiv(count, SUB * GRAN)
    for v in range(1, most // GRAN + 1):

        @pl.when(tiles == v)
        def _():
            center_tiles(q_ref, behind_ref, acc_ref, rows_ref, center, v * GRAN, near)


def own_kernel(count_ref, q_ref, out_ref, acc_ref, behind_ref, *, rows, cols):
    blocks = rows * cols
    lanes = q_ref.shape[2]

    def clear(b, _):
        acc_ref[b] = jnp.zeros((3, SUB, lanes), f32)
        out_ref[b] = jnp.zeros((SUB, lanes), f32)
        return 0

    lax.fori_loop(0, blocks, clear, 0)
    behind_ref[...] = jnp.zeros(behind_ref.shape, f32)

    def run(r, c, steps):
        center = r * cols + c
        near = [(center + sx * cols + sy, float(sx), float(sy), (sx, sy) != (0, 0)) for sx, sy in steps]
        center_block(q_ref, behind_ref, acc_ref, out_ref, center, count_ref[center], near)

    def one_row(r, _):
        run(r, 0, [(0, 1), (1, 0), (1, 1), (0, 0)])

        def middle(c, _):
            run(r, c, [(0, 1), (1, -1), (1, 0), (1, 1), (0, 0)])
            return 0

        lax.fori_loop(1, cols - 1, middle, 0)
        run(r, cols - 1, [(1, -1), (1, 0), (0, 0)])
        return 0

    lax.fori_loop(0, rows - 1, one_row, 0)

    def last_row(c, _):
        run(rows - 1, c, [(0, 1), (0, 0)])
        return 0

    lax.fori_loop(0, cols - 1, last_row, 0)
    run(rows - 1, cols - 1, [(0, 0)])
    sub = lax.broadcasted_iota(jnp.int32, (SUB, lanes), 0)

    def close(b, _):
        part = acc_ref[b]
        rows_sum = [jnp.sum(part[k], axis=0, keepdims=True) for k in range(3)]
        front = jnp.concatenate(rows_sum + [jnp.zeros((SUB - 3, lanes), f32)], axis=0)
        behind = out_ref[b]
        out_ref[b] = jnp.where(sub == 2, front + behind, front - behind)
        return 0

    lax.fori_loop(0, blocks, close, 0)


def halo_kernel(count_ref, index_ref, step_ref, q_ref, own_ref, wind_ref, out_ref, peak_ref, acc_ref, *, rows, cols):
    lanes = q_ref.shape[2]

    def clear(b, _):
        acc_ref[b] = jnp.zeros((3, SUB, lanes), f32)
        return 0

    lax.fori_loop(0, (rows + 2) * (cols + 2), clear, 0)

    def one_center(n, _):
        center = index_ref[4 * n]
        near = [
            (index_ref[4 * n + 1 + k], step_ref[6 * n + 2 * k], step_ref[6 * n + 2 * k + 1], False)
            for k in range(3)
        ]
        center_block(q_ref, None, acc_ref, None, center, count_ref[center], near)
        return 0

    lax.fori_loop(0, 2 * (rows + cols + 2), one_center, 0)
    peak_ref[...] = jnp.zeros(peak_ref.shape, f32)

    def close_row(r, _):
        def close(c, _):
            b = r * cols + c
            e = (r + 1) * (cols + 2) + c + 1
            part = acc_ref[e]
            total = [jnp.sum(part[k], axis=0, keepdims=True) + own_ref[b, k : k + 1, :] for k in range(3)]
            mass = q_ref[e, 6:7, :]
            live = mass > 0.0
            scale = grad_coef / jnp.where(live, mass, 1.0)
            here = pl.ds(b, 1)
            acc_x = jnp.where(live, wind_ref[0, here, :] - scale * total[0], 0.0)
            acc_y = jnp.where(live, wind_ref[1, here, :] - scale * total[1], 0.0)
            out_ref[0, here, :] = acc_x
            out_ref[1, here, :] = acc_y
            out_ref[2, here, :] = jnp.where(live, scale * total[2], 0.0)
            peak_ref[0:1] = jnp.maximum(peak_ref[0:1], acc_x * acc_x + acc_y * acc_y)
            return 0

        lax.fori_loop(0, cols, close, 0)
        return 0

    lax.fori_loop(0, rows, close_row, 0)


def halo_lists(rows, cols):
    wide = cols + 2
    index, step = [], []

    def add(r, c, steps):
        index.extend([r * wide + c] + [(r + sx) * wide + c + sy for sx, sy in steps])
        for sx, sy in steps:
            step.extend([sx, sy])

    for c in range(wide):
        add(0, c, [(1, -1), (1, 0), (1, 1)])
        add(rows + 1, c, [(-1, -1), (-1, 0), (-1, 1)])
    for r in range(1, rows + 1):
        add(r, 0, [(-1, 1), (0, 1), (1, 1)])
        add(r, cols + 1, [(-1, -1), (0, -1), (1, -1)])
    return np.asarray(index, np.int32), np.asarray(step, np.float32)


def spaces(smem, vmem):
    return [pl.BlockSpec(memory_space=pltpu.SMEM)] * smem + [pl.BlockSpec(memory_space=pltpu.VMEM)] * vmem


def own_forces(counts, fields, rows, cols):
    blocks, _, lanes = fields.shape
    return pl.pallas_call(
        functools.partial(own_kernel, rows=rows, cols=cols),
        out_shape=jax.ShapeDtypeStruct((blocks, SUB, lanes), f32),
        in_specs=spaces(1, 1),
        out_specs=pl.BlockSpec(memory_space=pltpu.VMEM),
        scratch_shapes=[pltpu.VMEM((blocks, 3, SUB, lanes), f32), pltpu.VMEM((3, lanes, lanes), f32)],
        compiler_params=pltpu.CompilerParams(vmem_limit_bytes=VMEM_LIMIT),
        cost_estimate=pl.CostEstimate(flops=400_000_000, bytes_accessed=2_000_000, transcendentals=20_000_000),
    )(counts, fields)


def halo_forces(counts, extended, own, wind, rows, cols):
    blocks = rows * cols
    lanes = extended.shape[2]
    index, step = halo_lists(rows, cols)
    return pl.pallas_call(
        functools.partial(halo_kernel, rows=rows, cols=cols),
        out_shape=(
            jax.ShapeDtypeStruct((3, blocks, lanes), f32),
            jax.ShapeDtypeStruct((SUB, lanes), f32),
        ),
        in_specs=spaces(3, 3),
        out_specs=tuple(spaces(0, 2)),
        scratch_shapes=[pltpu.VMEM(((rows + 2) * (cols + 2), 3, SUB, lanes), f32)],
        compiler_params=pltpu.CompilerParams(vmem_limit_bytes=VMEM_LIMIT),
    )(counts, jnp.asarray(index), jnp.asarray(step), extended, own, wind)


def pick_kernel(slot_ref, keep_ref, table_ref, out_ref):
    count, blocks, lanes = table_ref.shape
    for g in range(slot_ref.shape[0] // SUB):
        here = slice(g * SUB, g * SUB + SUB)
        slots = slot_ref[here]
        block_of = slots // lanes
        lane_of = slots % lanes

        def one(b, picked):
            hit = block_of == b
            rows = [jnp.broadcast_to(table_ref[k, pl.ds(b, 1), :], (SUB, lanes)) for k in range(count)]
            got = [jnp.take_along_axis(row, lane_of, axis=1) for row in rows]
            return tuple(jnp.where(hit, new, old) for new, old in zip(got, picked))

        start = (jnp.zeros((SUB, lanes), f32),) * count
        picked = lax.fori_loop(0, blocks, one, start, unroll=8)
        for k in range(count):
            out_ref[k, here] = picked[k] * keep_ref[here]


def pick(slots, keep, table, ways):
    count = table.shape[0]
    rows, lanes = slots.shape
    picked = pl.pallas_call(
        pick_kernel,
        out_shape=jax.ShapeDtypeStruct((count, rows, lanes), f32),
        in_specs=spaces(0, 3),
        out_specs=pl.BlockSpec(memory_space=pltpu.VMEM),
        compiler_params=pltpu.CompilerParams(vmem_limit_bytes=VMEM_LIMIT),
    )(slots, keep, table)
    return picked.reshape(count, ways, rows // ways, lanes)


def send_on(picked):
    return [
        passed_along(picked[:, 0], "shore", 1),
        passed_along(picked[:, 1], "shore", -1),
        passed_along(picked[:, 2], "cross", 1),
        passed_along(picked[:, 3], "cross", -1),
    ]


def time_step(peak_acc, peak_speed):
    return 0.25 * smooth / (sound_speed + peak_speed + jnp.sqrt(smooth * peak_acc))


def body(
    positions,
    velocity,
    density,
    particle_mass,
    cell_count,
    wind_seed,
    wind_table,
    migrant_slot,
    migrant_count,
):
    _, rows, cols, lanes = positions.shape
    blocks = rows * cols
    slot_ids = jnp.arange(lanes, dtype=jnp.int32)
    alive = slot_ids[None, None, :] < cell_count[:, :, None]
    live = alive.astype(f32)
    live_mass = particle_mass * live
    fields = jnp.stack(
        [
            positions[0],
            positions[1],
            velocity[0],
            velocity[1],
            density,
            pressure_ratio(density),
            live_mass,
            live,
        ],
        axis=2,
    )
    above = passed_along(fields[rows - 1 :], "shore", 1)
    below = passed_along(fields[:1], "shore", -1)
    tall = jnp.concatenate([above, fields, below], axis=0)
    left = passed_along(tall[:, cols - 1 :], "cross", 1)
    right = passed_along(tall[:, :1], "cross", -1)
    extended = jnp.concatenate([left, tall, right], axis=1)
    extended = extended.reshape((rows + 2) * (cols + 2), SUB, lanes)
    wide_count = jnp.sum(extended[:, 7] > 0.0, axis=1, dtype=jnp.int32)

    own = own_forces(cell_count.reshape(-1), fields.reshape(blocks, SUB, lanes), rows, cols)

    level_ids = jnp.arange(wind_table.shape[1], dtype=jnp.int32)
    one_hot = (wind_seed[None] == level_ids[:, None, None, None]).astype(f32)
    windage = jnp.einsum("cl,lxyp->cxyp", wind_table, one_hot, precision=lax.Precision.HIGHEST)

    ways = migrant_slot.shape[2]
    width = migrant_slot.shape[3]
    slots = migrant_slot.reshape(-1, lanes)
    keep = jnp.arange(width, dtype=jnp.int32)[None, :] < migrant_count.reshape(ways, 1)
    keep = keep.astype(f32).reshape(-1, lanes)
    early = jnp.stack(
        [
            positions[0] * live,
            positions[1] * live,
            velocity[0] * live,
            velocity[1] * live,
            density * live,
            live_mass,
        ]
    )
    came_early = send_on(pick(slots, keep, early.reshape(-1, blocks, lanes), ways))

    late, peak = halo_forces(
        wide_count, extended, own, windage.reshape(2, blocks, lanes), rows, cols
    )
    speed_sq = velocity[0] * velocity[0] + velocity[1] * velocity[1]
    peaks = jnp.stack([jnp.max(peak), jnp.max(speed_sq * live)])
    peaks = jnp.sqrt(everywhere_max(peaks))
    delta_t = time_step(peaks[0], peaks[1])
    came_late = send_on(pick(slots, keep, late, ways))

    acceleration = late[:2].reshape(2, rows, cols, lanes)
    rate = late[2].reshape(rows, cols, lanes)
    new_velocity = (velocity + delta_t * acceleration) * live[None]
    new_position = (positions + delta_t * new_velocity) * live[None]
    new_density = (density + delta_t * rate) * live
    state_next = jnp.concatenate([new_position, new_velocity, new_density[None], acceleration])

    at = jnp.stack(came_early)
    on = jnp.stack(came_late)
    moved_velocity = at[:, 2:4] + delta_t * on[:, 0:2]
    moved_position = at[:, 0:2] + delta_t * moved_velocity
    moved_density = at[:, 4:5] + delta_t * on[:, 2:3]
    arrivals = jnp.concatenate(
        [moved_position, moved_velocity, moved_density, at[:, 5:6], on[:, 0:2]], axis=1
    )
    return (state_next, arrivals.reshape(1, 1, ways, arrivals.shape[1], width))


def solution(mesh):
    in_specs = (
        P(None, "shore", "cross", None),
        P(None, "shore", "cross", None),
        P("shore", "cross", None),
        P("shore", "cross", None),
        P("shore", "cross"),
        P("shore", "cross", None),
        P(),
        P("shore", "cross", None, None),
        P("shore", "cross", None),
    )
    out_specs = (P(None, "shore", "cross", None), P("shore", "cross", None, None, None))
    return jax.shard_map(body, mesh=mesh, in_specs=in_specs, out_specs=out_specs, check_vma=False)
```

time: 306 us -> 226 us (0.74)
  Pallas kernels: 0 us -> 142 us
  other arithmetic: 131 us -> 15.2 us
  local copies, waits for them, and re-layouts: 51.9 us -> 7.22 us
  blocking collectives: 40.7 us -> 0 us
  loops' own time: 33.5 us -> 0 us
  starting transfers between devices: 30.7 us -> 39 us
  waiting for transfers between devices: 13.9 us -> 18.4 us
    pallas_call x0 -> x4, Pallas kernels: none -> 142 us  [the longest x1 95.3 us: own_forces(): pl.pallas_call(functools.partial(own_kernel, rows=rows, cols=cols), out_s...]
    reduce_sum x64 -> x1, other arithmetic: 123 us -> 3.28 us  [body(): wide_count = jnp.sum(extended[:, 7] > 0.0, axis=1, dtype=jnp.int32)]
    pmax x1 -> x0, blocking collectives: 40.7 us -> none  [body(): lax.pmax((local_acc, local_speed), ('shore', 'cross'))]
    another operation x1 -> x0, loops' own time: 33.5 us -> none  [half_forces(): lax.map(one_row, jnp.arange(row_count, dtype=jnp.int32))]
    gather x2 -> x0, local copies, waits for them, and re-layouts: 30.1 us -> none  [pick_migrants(): picked = jnp.take(flattened, slot_list.reshape(-1), axis=1)]
    ppermute x7 -> x12, starting transfers between devices: 19.3 us -> 34.6 us  [passed_along(): return lax.ppermute(array, axis, pairs)]
    dynamic_slice x16 -> x0, local copies, waits for them, and re-layouts: 9.38 us -> none  [half_forces(): lax.map(one_row, jnp.arange(row_count, dtype=jnp.int32))]
    ppermute x4 -> x5, waiting for transfers between devices: 4.83 us -> 13.2 us  [everywhere_max(): array = jnp.maximum(array, lax.ppermute(array, axis, pairs))]
  transfers between devices with their start and end apart: 11 -> 17, of which waited for: 6 -> 6; matrix products, arithmetic and copies ran while one was open for 1% -> 4% of each run, Pallas kernels for 0% -> 48%
where the time goes in v1:
time: 226 us; the launch traced here: 225 us
  Pallas kernels  142 us (63%)
  starting transfers between devices  39 us (17%)
  waiting for transfers between devices  18.4 us (8%)
  other arithmetic  15.2 us (7%)
  local copies, waits for them, and re-layouts  7.22 us (3%)
  between operations  2.66 us (1%)
    pallas_call x1, Pallas kernels, own_forces(): pl.pallas_call(functools.partial(own_kernel, rows=rows, cols=cols), out_s...  95.3 us
    ppermute x12, starting transfers between devices, passed_along(): return lax.ppermute(array, axis, pairs)  34.6 us
    pallas_call x2, Pallas kernels, pick(): pl.pallas_call(pick_kernel, out_shape=jax.ShapeDtypeStruct((count, rows,...  24.2 us
    pallas_call x1, Pallas kernels, halo_forces(): pl.pallas_call(functools.partial(halo_kernel, rows=rows, cols=cols), out_...  22.5 us
    ppermute x5, waiting for transfers between devices, everywhere_max(): array = jnp.maximum(array, lax.ppermute(array, axis, pairs))  13.2 us
    ppermute x12, waiting for transfers between devices, passed_along(): return lax.ppermute(array, axis, pairs)  5.18 us
    unnamed x10, other arithmetic  4.68 us
  transfers between devices with their start and end apart: 17, of which 6 were waited for; matrix products, arithmetic and copies ran while one was open for 4% of the time, Pallas kernels for 48%

profile of v1, /device:TPU:6, one launch (start us, length us, event | category | flops | bytes accessed | tf_op | source)
XLA Modules:
  0.0 224.8 jit_solution(17044072126357525170)
XLA Ops:
  9.8 1.9 collective-permute-start
  11.8 3.6 %collective-permute-start.1 = (f32[1,8,8,128]{3,1,0,2:T(8,128)S(1)}, f32[1,8,8,128]{3,1,0,2:T(8,128)S(1)}, u32[]{:S(2)}, u32[]{:S(2)}) collective-permute-start(f32[1,8,8,128]{3,1,0,2:T(8,128)S(1)} %get-tuple-element.13), channel_id=1, source_target_pairs={{8,0},{16,8},{24,16},{9,1},{17,9},{25,17},{10,2},{18,10},{26,18},{... | collective-permute-start | bytes 98312 | tf_op jit(solution)/shard_map/ppermute | solution.py:24
  15.7 13.5 %shard_map.124 = f32[6,56,128]{2,1,0:T(8,128)S(1)} custom-call(s32[56,128]{1,0:T(8,128)S(1)} %reshape.129.slot_ref, f32[56,128]{1,0:T(8,128)S(1)} %compare_convert_fusion.2.keep_ref, f32[6,128,128]{2,1,0:T(8,128)S(1)} %get-tuple-element.6.table_ref), custom_call_target="tpu_custom_call" | custom-call | tf_op jit(solution)/shard_map/pallas_call | solution.py:291
  29.3 1.9 collective-permute-start.9
  31.2 3.6 %collective-permute-start.10 = (f32[6,14,128]{2,1,0:T(8,128)S(1)}, f32[6,14,128]{2,1,0:T(8,128)S(1)}, u32[]{:S(2)}, u32[]{:S(2)}) collective-permute-start(f32[6,14,128]{2,1,0:T(8,128)S(1)} %get-tuple-element.15), channel_id=1, source_target_pairs={{8,0},{16,8},{24,16},{9,1},{17,9},{25,17},{10,2},{18,10},{26,18},{... | collective-permute-start | bytes 129032 | tf_op jit(solution)/shard_map/ppermute | solution.py:24
  34.9 3.4 %collective-permute-start.11 = (f32[6,14,128]{2,1,0:T(8,128)S(1)}, f32[6,14,128]{2,1,0:T(8,128)S(1)}, u32[]{:S(2)}, u32[]{:S(2)}) collective-permute-start(f32[6,14,128]{2,1,0:T(8,128)S(1)} %get-tuple-element.17), channel_id=1, source_target_pairs={{0,1},{1,2},{2,3},{3,4},{4,5},{5,6},{6,7},{8,9},{9,10},{10,11},{11... | collective-permute-start | bytes 129032 | tf_op jit(solution)/shard_map/ppermute | solution.py:24
  40.8 95.3 %shard_map.122.own_ref = f32[128,8,128]{2,1,0:T(8,128)S(1)} custom-call(s32[128]{0:T(128)S(1)} %reshape.126.count_ref, f32[128,8,128]{2,1,0:T(8,128)S(1)} %stack.100.q_ref), custom_call_target="tpu_custom_call" | custom-call | flops 400000000 | bytes 2000000 | tf_op jit(solution)/shard_map/pallas_call | solution.py:240
  136.0 2.4 %collective-permute-start.12 = (f32[6,14,128]{2,1,0:T(8,128)S(1)}, f32[6,14,128]{2,1,0:T(8,128)S(1)}, u32[]{:S(2)}, u32[]{:S(2)}) collective-permute-start(f32[6,14,128]{2,1,0:T(8,128)S(1)} %get-tuple-element.16), channel_id=1, source_target_pairs={{1,0},{2,1},{3,2},{4,3},{5,4},{6,5},{7,6},{9,8},{10,9},{11,10},{12... | collective-permute-start | bytes 129032 | tf_op jit(solution)/shard_map/ppermute | solution.py:24
  138.5 4.4 %collective-permute-start.2 = (f32[18,1,8,128]{3,1,0,2:T(1,128)S(1)}, f32[18,1,8,128]{3,1,0,2:T(1,128)S(1)}, u32[]{:S(2)}, u32[]{:S(2)}) collective-permute-start(f32[18,1,8,128]{3,1,0,2:T(1,128)S(1)} %get-tuple-element.10), channel_id=1, source_target_pairs={{0,1},{1,2},{2,3},{3,4},{4,5},{5,6},{6,7},{8,9},{9,10},{10,11},{11... | collective-permute-start | bytes 221192 | tf_op jit(solution)/shard_map/ppermute | solution.py:24
  142.9 1.9 collective-permute-start.3
  144.9 5.2 %collective-permute-done.3 = f32[18,1,8,128]{3,1,0,2:T(1,128)S(1)} collective-permute-done((f32[18,1,8,128]{3,1,0,2:T(1,128)S(1)}, f32[18,1,8,128]{3,1,0,2:T(1,128)S(1)}, u32[]{:S(2)}, u32[]{:S(2)}) %collective-permute-start.3) | collective-permute-done | bytes 73760 | tf_op jit(solution)/shard_map/ppermute | solution.py:24
  150.8 3.3 %fusion.1.count_ref = s32[180]{0:T(256)S(1)} fusion(f32[180,8,128]{2,1,0:T(8,128)S(1)} %bitcast.103), kind=kLoop, calls=%fused_computation.15 | loop fusion | flops 68940 | bytes 92880 | tf_op jit(solution)/shard_map/reduce_sum | solution.py:351
  154.1 22.5 %shard_map.123 = (f32[3,128,128]{2,1,0:T(8,128)S(1)}, f32[8,128]{1,0:T(8,128)S(1)}) custom-call(s32[180]{0:T(256)S(1)} %fusion.1.count_ref, s32[208]{0:T(256)S(1)} %copy-done.2, f32[312]{0:T(512)S(1)} %copy-done.1, f32[180,8,128]{2,1,0:T(8,128)S(1)} %bitcast.104, f32[128,8,128]{2,1,0:T(8,128)S(1)} %shard_map.122.own_ref, f32[2,128,128]{2,1,0:T(8,128)S(1)} %bitcast.105), custom_call_target="tpu_custom_call" | custom-call | tf_op jit(solution)/shard_map/pallas_call | solution.py:255
  176.6 10.7 %shard_map.125 = f32[3,56,128]{2,1,0:T(8,128)S(1)} custom-call(s32[56,128]{1,0:T(8,128)S(1)} %reshape.129.slot_ref, f32[56,128]{1,0:T(8,128)S(1)} %compare_convert_fusion.2.keep_ref, f32[3,128,128]{2,1,0:T(8,128)S(1)} %get-tuple-element.5.table_ref), custom_call_target="tpu_custom_call" | custom-call | tf_op jit(solution)/shard_map/pallas_call | solution.py:291
  187.3 1.9 collective-permute-start.13
  189.2 3.6 %collective-permute-start.14 = (f32[3,14,128]{2,1,0:T(8,128)S(1)}, f32[3,14,128]{2,1,0:T(8,128)S(1)}, u32[]{:S(2)}, u32[]{:S(2)}) collective-permute-start(f32[3,14,128]{2,1,0:T(8,128)S(1)} %get-tuple-element.24), channel_id=1, source_target_pairs={{8,0},{16,8},{24,16},{9,1},{17,9},{25,17},{10,2},{18,10},{26,18},{... | collective-permute-start | bytes 64520 | tf_op jit(solution)/shard_map/ppermute | solution.py:24
  192.9 3.3 %collective-permute-start.15 = (f32[3,14,128]{2,1,0:T(8,128)S(1)}, f32[3,14,128]{2,1,0:T(8,128)S(1)}, u32[]{:S(2)}, u32[]{:S(2)}) collective-permute-start(f32[3,14,128]{2,1,0:T(8,128)S(1)} %get-tuple-element.23), channel_id=1, source_target_pairs={{0,1},{1,2},{2,3},{3,4},{4,5},{5,6},{6,7},{8,9},{9,10},{10,11},{11... | collective-permute-start | bytes 64520 | tf_op jit(solution)/shard_map/ppermute | solution.py:24
  196.2 2.5 %collective-permute-start.16 = (f32[3,14,128]{2,1,0:T(8,128)S(1)}, f32[3,14,128]{2,1,0:T(8,128)S(1)}, u32[]{:S(2)}, u32[]{:S(2)}) collective-permute-start(f32[3,14,128]{2,1,0:T(8,128)S(1)} %get-tuple-element.25), channel_id=1, source_target_pairs={{1,0},{2,1},{3,2},{4,3},{5,4},{6,5},{7,6},{9,8},{10,9},{11,10},{12... | collective-permute-start | bytes 64520 | tf_op jit(solution)/shard_map/ppermute | solution.py:24
  200.7 3.5 %collective-permute-done.4 = f32[2]{0:T(128)S(1)} collective-permute-done((f32[2]{0:T(128)S(1)}, f32[2]{0:T(128)S(1)}, u32[]{:S(2)}, u32[]{:S(2)}) %collective-permute-start.4) | collective-permute-done | bytes 40 | tf_op jit(solution)/shard_map/ppermute | solution.py:36
  205.6 3.4 %collective-permute-start.5 = (f32[2]{0:T(128)S(1)}, f32[2]{0:T(128)S(1)}, u32[]{:S(2)}, u32[]{:S(2)}) collective-permute-start(f32[2]{0:T(128)S(1)} %fusion.19), channel_id=1, source_target_pairs={{0,2},{1,3},{2,0},{3,1},{4,6},{5,7},{6,4},{7,5},{8,10},{9,11},{10,... | collective-permute-start | bytes 32 | tf_op jit(solution)/shard_map/ppermute | solution.py:36
  209.0 1.5 collective-permute-done.5
  210.5 1.4 fusion.20
  212.9 3.5 %collective-permute-done.6 = f32[2]{0:T(128)S(1)} collective-permute-done((f32[2]{0:T(128)S(1)}, f32[2]{0:T(128)S(1)}, u32[]{:S(2)}, u32[]{:S(2)}) %collective-permute-start.6) | collective-permute-done | bytes 40 | tf_op jit(solution)/shard_map/ppermute | solution.py:36
  217.5 3.5 %collective-permute-done.8 = f32[2]{0:T(128)S(1)} collective-permute-done((f32[2]{0:T(128)S(1)}, f32[2]{0:T(128)S(1)}, u32[]{:S(2)}, u32[]{:S(2)}) %collective-permute-start.8) | collective-permute-done | bytes 40 | tf_op jit(solution)/shard_map/ppermute | solution.py:36
  (95 shorter events, 20.3 us)
Async XLA Ops:
  0.6 38.8 %copy-start = (f32[2,16]{1,0:T(2,128)S(1)}, f32[2,16]{1,0:T(2,128)}, u32[]{:S(2)}) copy-start(f32[2,16]{1,0:T(2,128)} %param.17) | copy-start | bytes 388
  0.7 8.9 %copy-start.6 = (f32[16,8,128]{2,1,0:T(8,128)S(1)}, f32[16,8,128]{2,1,0:T(8,128)}, u32[]{:S(2)}) copy-start(f32[16,8,128]{2,1,0:T(8,128)} %param.14) | copy-start | bytes 196612
  0.7 14.8 %copy-start.8 = (s32[1,1,4]{2,1,0:T(1,128)S(1)}, s32[1,1,4]{2,1,0:T(1,128)}, u32[]{:S(2)}) copy-start(s32[1,1,4]{2,1,0:T(1,128)} %param.19) | copy-start | bytes 52
  0.7 14.9 %copy-start.7 = (s32[1,1,4,1792]{3,2,1,0:T(4,128)S(1)}, s32[1,1,4,1792]{3,2,1,0:T(4,128)}, u32[]{:S(2)}) copy-start(s32[1,1,4,1792]{3,2,1,0:T(4,128)} %param.18) | copy-start | bytes 86020
  9.6 28.8 %copy-start.3 = (f32[2,16,8,128]{3,2,1,0:T(8,128)S(1)}, f32[2,16,8,128]{3,2,1,0:T(8,128)}, u32[]{:S(2)}) copy-start(f32[2,16,8,128]{3,2,1,0:T(8,128)} %param.12) | copy-start | bytes 393220
  9.6 28.8 %copy-start.5 = (f32[2,16,8,128]{3,2,1,0:T(8,128)S(1)}, f32[2,16,8,128]{3,2,1,0:T(8,128)}, u32[]{:S(2)}) copy-start(f32[2,16,8,128]{3,2,1,0:T(8,128)} %param.11) | copy-start | bytes 393220
  9.8 126.2 %collective-permute-start = (f32[1,8,8,128]{3,1,0,2:T(8,128)S(1)}, f32[1,8,8,128]{3,1,0,2:T(8,128)S(1)}, u32[]{:S(2)}, u32[]{:S(2)}) collective-permute-start(f32[1,8,8,128]{3,1,0,2:T(8,128)S(1)} %get-tuple-element.12), channel_id=1, source_target_pairs={{0,8},{8,16},{16,24},{1,9},{9,17},{17,25},{2,10},{10,18},{18,26},{... | collective-permute-start | bytes 98312 | tf_op jit(solution)/shard_map/ppermute | solution.py:24
  11.8 126.7 %collective-permute-start.1 = (f32[1,8,8,128]{3,1,0,2:T(8,128)S(1)}, f32[1,8,8,128]{3,1,0,2:T(8,128)S(1)}, u32[]{:S(2)}, u32[]{:S(2)}) collective-permute-start(f32[1,8,8,128]{3,1,0,2:T(8,128)S(1)} %get-tuple-element.13), channel_id=1, source_target_pairs={{8,0},{16,8},{24,16},{9,1},{17,9},{25,17},{10,2},{18,10},{26,18},{... | collective-permute-start | bytes 98312 | tf_op jit(solution)/shard_map/ppermute | solution.py:24
  15.7 23.8 %copy-start.9 = (s32[16,8,128]{2,1,0:T(8,128)S(1)}, s32[16,8,128]{2,1,0:T(8,128)}, u32[]{:S(2)}) copy-start(s32[16,8,128]{2,1,0:T(8,128)} %param.16) | copy-start | bytes 196612
  29.3 113.6 %collective-permute-start.9 = (f32[6,14,128]{2,1,0:T(8,128)S(1)}, f32[6,14,128]{2,1,0:T(8,128)S(1)}, u32[]{:S(2)}, u32[]{:S(2)}) collective-permute-start(f32[6,14,128]{2,1,0:T(8,128)S(1)} %get-tuple-element.14), channel_id=1, source_target_pairs={{0,8},{8,16},{16,24},{1,9},{9,17},{17,25},{2,10},{10,18},{18,26},{... | collective-permute-start | bytes 129032 | tf_op jit(solution)/shard_map/ppermute | solution.py:24
  31.2 113.6 %collective-permute-start.10 = (f32[6,14,128]{2,1,0:T(8,128)S(1)}, f32[6,14,128]{2,1,0:T(8,128)S(1)}, u32[]{:S(2)}, u32[]{:S(2)}) collective-permute-start(f32[6,14,128]{2,1,0:T(8,128)S(1)} %get-tuple-element.15), channel_id=1, source_target_pairs={{8,0},{16,8},{24,16},{9,1},{17,9},{25,17},{10,2},{18,10},{26,18},{... | collective-permute-start | bytes 129032 | tf_op jit(solution)/shard_map/ppermute | solution.py:24
  34.9 110.0 %collective-permute-start.11 = (f32[6,14,128]{2,1,0:T(8,128)S(1)}, f32[6,14,128]{2,1,0:T(8,128)S(1)}, u32[]{:S(2)}, u32[]{:S(2)}) collective-permute-start(f32[6,14,128]{2,1,0:T(8,128)S(1)} %get-tuple-element.17), channel_id=1, source_target_pairs={{0,1},{1,2},{2,3},{3,4},{4,5},{5,6},{6,7},{8,9},{9,10},{10,11},{11... | collective-permute-start | bytes 129032 | tf_op jit(solution)/shard_map/ppermute | solution.py:24
  136.0 8.8 %collective-permute-start.12 = (f32[6,14,128]{2,1,0:T(8,128)S(1)}, f32[6,14,128]{2,1,0:T(8,128)S(1)}, u32[]{:S(2)}, u32[]{:S(2)}) collective-permute-start(f32[6,14,128]{2,1,0:T(8,128)S(1)} %get-tuple-element.16), channel_id=1, source_target_pairs={{1,0},{2,1},{3,2},{4,3},{5,4},{6,5},{7,6},{9,8},{10,9},{11,10},{12... | collective-permute-start | bytes 129032 | tf_op jit(solution)/shard_map/ppermute | solution.py:24
  138.5 6.4 %collective-permute-start.2 = (f32[18,1,8,128]{3,1,0,2:T(1,128)S(1)}, f32[18,1,8,128]{3,1,0,2:T(1,128)S(1)}, u32[]{:S(2)}, u32[]{:S(2)}) collective-permute-start(f32[18,1,8,128]{3,1,0,2:T(1,128)S(1)} %get-tuple-element.10), channel_id=1, source_target_pairs={{0,1},{1,2},{2,3},{3,4},{4,5},{5,6},{6,7},{8,9},{9,10},{10,11},{11... | collective-permute-start | bytes 221192 | tf_op jit(solution)/shard_map/ppermute | solution.py:24
  142.9 7.1 %collective-permute-start.3 = (f32[18,1,8,128]{3,1,0,2:T(1,128)S(1)}, f32[18,1,8,128]{3,1,0,2:T(1,128)S(1)}, u32[]{:S(2)}, u32[]{:S(2)}) collective-permute-start(f32[18,1,8,128]{3,1,0,2:T(1,128)S(1)} %get-tuple-element.11), channel_id=1, source_target_pairs={{1,0},{2,1},{3,2},{4,3},{5,4},{6,5},{7,6},{9,8},{10,9},{11,10},{12... | collective-permute-start | bytes 221192 | tf_op jit(solution)/shard_map/ppermute | solution.py:24
  187.3 36.7 %collective-permute-start.13 = (f32[3,14,128]{2,1,0:T(8,128)S(1)}, f32[3,14,128]{2,1,0:T(8,128)S(1)}, u32[]{:S(2)}, u32[]{:S(2)}) collective-permute-start(f32[3,14,128]{2,1,0:T(8,128)S(1)} %get-tuple-element.22), channel_id=1, source_target_pairs={{0,8},{8,16},{16,24},{1,9},{9,17},{17,25},{2,10},{10,18},{18,26},{... | collective-permute-start | bytes 64520 | tf_op jit(solution)/shard_map/ppermute | solution.py:24
  189.2 34.7 %collective-permute-start.14 = (f32[3,14,128]{2,1,0:T(8,128)S(1)}, f32[3,14,128]{2,1,0:T(8,128)S(1)}, u32[]{:S(2)}, u32[]{:S(2)}) collective-permute-start(f32[3,14,128]{2,1,0:T(8,128)S(1)} %get-tuple-element.24), channel_id=1, source_target_pairs={{8,0},{16,8},{24,16},{9,1},{17,9},{25,17},{10,2},{18,10},{26,18},{... | collective-permute-start | bytes 64520 | tf_op jit(solution)/shard_map/ppermute | solution.py:24
  192.9 31.1 %collective-permute-start.15 = (f32[3,14,128]{2,1,0:T(8,128)S(1)}, f32[3,14,128]{2,1,0:T(8,128)S(1)}, u32[]{:S(2)}, u32[]{:S(2)}) collective-permute-start(f32[3,14,128]{2,1,0:T(8,128)S(1)} %get-tuple-element.23), channel_id=1, source_target_pairs={{0,1},{1,2},{2,3},{3,4},{4,5},{5,6},{6,7},{8,9},{9,10},{10,11},{11... | collective-permute-start | bytes 64520 | tf_op jit(solution)/shard_map/ppermute | solution.py:24
  196.2 27.8 %collective-permute-start.16 = (f32[3,14,128]{2,1,0:T(8,128)S(1)}, f32[3,14,128]{2,1,0:T(8,128)S(1)}, u32[]{:S(2)}, u32[]{:S(2)}) collective-permute-start(f32[3,14,128]{2,1,0:T(8,128)S(1)} %get-tuple-element.25), channel_id=1, source_target_pairs={{1,0},{2,1},{3,2},{4,3},{5,4},{6,5},{7,6},{9,8},{10,9},{11,10},{12... | collective-permute-start | bytes 64520 | tf_op jit(solution)/shard_map/ppermute | solution.py:24
  200.7 3.5 %collective-permute-start.4 = (f32[2]{0:T(128)S(1)}, f32[2]{0:T(128)S(1)}, u32[]{:S(2)}, u32[]{:S(2)}) collective-permute-start(f32[2]{0:T(128)S(1)} %pad_maximum_fusion.7), channel_id=1, source_target_pairs={{0,1},{1,0},{2,3},{3,2},{4,5},{5,4},{6,7},{7,6},{8,9},{9,8},{10,11... | collective-permute-start | bytes 32 | tf_op jit(solution)/shard_map/ppermute | solution.py:36
  205.6 4.9 %collective-permute-start.5 = (f32[2]{0:T(128)S(1)}, f32[2]{0:T(128)S(1)}, u32[]{:S(2)}, u32[]{:S(2)}) collective-permute-start(f32[2]{0:T(128)S(1)} %fusion.19), channel_id=1, source_target_pairs={{0,2},{1,3},{2,0},{3,1},{4,6},{5,7},{6,4},{7,5},{8,10},{9,11},{10,... | collective-permute-start | bytes 32 | tf_op jit(solution)/shard_map/ppermute | solution.py:36
  211.9 4.4 %collective-permute-start.6 = (f32[2]{0:T(128)S(1)}, f32[2]{0:T(128)S(1)}, u32[]{:S(2)}, u32[]{:S(2)}) collective-permute-start(f32[2]{0:T(128)S(1)} %fusion.20), channel_id=1, source_target_pairs={{0,4},{1,5},{2,6},{3,7},{4,0},{5,1},{6,2},{7,3},{8,12},{9,13},{10,... | collective-permute-start | bytes 32 | tf_op jit(solution)/shard_map/ppermute | solution.py:36
  216.4 1.1 collective-permute-start.7
  217.5 3.5 %collective-permute-start.8 = (f32[2]{0:T(128)S(1)}, f32[2]{0:T(128)S(1)}, u32[]{:S(2)}, u32[]{:S(2)}) collective-permute-start(f32[2]{0:T(128)S(1)} %max.18), channel_id=1, source_target_pairs={{0,16},{8,24},{16,0},{24,8},{1,17},{9,25},{17,1},{25,9},{2,18},{10... | collective-permute-start | bytes 32 | tf_op jit(solution)/shard_map/ppermute | solution.py:36
  (3 other events, 16.4 us)

commit v2 on v1

v2 whole, which is shorter than its diff:
```python
import functools

import jax
import jax.numpy as jnp
import numpy as np
from jax import lax
from jax.experimental import pallas as pl
from jax.experimental.pallas import tpu as pltpu
from jax.sharding import PartitionSpec as P

sound_speed = 10.0
smooth = 0.5
kernel_norm = 7.0 / (4.0 * 3.141592653589793 * smooth * smooth)
grad_coef = -5.0 * kernel_norm / (smooth * smooth)
f32 = jnp.float32
SUB = 8
GRAN = 2
VMEM_LIMIT = 48 * 1024 * 1024


def passed_along(array, axis, by):
    peers = lax.axis_size(axis)
    pairs = [(i, i + by) for i in range(peers) if 0 <= i + by < peers]
    return lax.ppermute(array, axis, pairs)


def everywhere_max(array):
    for axis in ("cross", "shore"):
        peers = lax.axis_size(axis)
        step = 1
        while step < peers:
            if peers & (peers - 1) == 0:
                pairs = [(i, i ^ step) for i in range(peers)]
            else:
                pairs = [(i, (i + step) % peers) for i in range(peers)]
            array = jnp.maximum(array, lax.ppermute(array, axis, pairs))
            step *= 2
    return array


def pressure_ratio(density):
    cube = density * density * density
    seventh = cube * cube * density
    pressure = sound_speed * sound_speed / 7.0 * (seventh - 1.0)
    return pressure / (density * density)


def pair_terms(own, near):
    dx = own[0] - near[0]
    dy = own[1] - near[1]
    dist_sq = dx * dx + dy * dy
    guarded = jnp.maximum(dist_sq, 1e-30)
    radius = guarded * lax.rsqrt(guarded)
    falloff = jnp.maximum(1.0 - radius, 0.0)
    weight = (falloff * falloff) * (falloff * (own[6] * near[6]))
    approach = (own[2] - near[2]) * dx + (own[3] - near[3]) * dy
    bottom = (dist_sq + 0.01 * smooth * smooth) * (own[4] + near[4])
    total = (own[5] + near[5]) - jnp.minimum(approach, 0.0) * pltpu.reciprocal(bottom, approx=True)
    shared = weight * total
    return shared * dx, shared * dy, weight * approach


def plus(total, term):
    return term if total is None else tuple(a + b for a, b in zip(total, term))


def center_tiles(q_ref, columns_ref, behind_ref, acc_ref, rows_ref, center, tiles, near, before):
    lanes = q_ref.shape[2]
    if before is not None:
        close_behind(behind_ref, rows_ref, before)
    others = []
    for block, _, step_x, step_y, _ in near:
        fields = [q_ref[block, k : k + 1, :] for k in range(7)]
        fields[0] = fields[0] + step_x
        fields[1] = fields[1] + step_y
        others.append([jnp.broadcast_to(f, (SUB, lanes)) for f in fields])
    sums = [None] * len(near)
    for t in range(tiles):
        tile = columns_ref[center, SUB * t : SUB * t + SUB, 0:SUB]
        mine = [jnp.broadcast_to(tile[:, k : k + 1], (SUB, lanes)) for k in range(7)]
        behind = None
        for n in range(len(near)):
            term = pair_terms(others[n], mine)
            sums[n] = plus(sums[n], term)
            if near[n][4]:
                behind = plus(behind, term)
        if behind is not None:
            for k in range(3):
                behind_ref[k, SUB * t : SUB * t + SUB, :] = behind[k]
    for n in range(len(near)):
        for k in range(3):
            acc_ref[near[n][1], k] = acc_ref[near[n][1], k] + sums[n][k]


def close_behind(behind_ref, rows_ref, center):
    lanes = behind_ref.shape[2]
    ones = jnp.ones((16, lanes), jnp.bfloat16)
    dims = (((1,), (1,)), ((), ()))
    sub = lax.broadcasted_iota(jnp.int32, (SUB, lanes), 0)
    total = jnp.zeros((SUB, lanes), f32)
    for k in range(3):
        part = behind_ref[k]
        high = part.astype(jnp.bfloat16)
        low = (part - high.astype(f32)).astype(jnp.bfloat16)
        row = sum(
            lax.dot_general(ones, piece, dims, preferred_element_type=f32) for piece in (high, low)
        )
        total = jnp.where(sub == k, row[:SUB], total)
    rows_ref[center] = total


def center_block(q_ref, columns_ref, behind_ref, acc_ref, rows_ref, center, count, near, before):
    most = q_ref.shape[2] // SUB
    tiles = pl.cdiv(count, SUB * GRAN)
    for v in range(0 if before is not None else 1, most // GRAN + 1):

        @pl.when(tiles == v)
        def _():
            if v == 0:
                close_behind(behind_ref, rows_ref, before)
                behind_ref[...] = jnp.zeros(behind_ref.shape, f32)
            else:
                center_tiles(
                    q_ref, columns_ref, behind_ref, acc_ref, rows_ref, center, v * GRAN, near, before
                )


def turn_columns(q_ref, columns_ref, blocks):
    def turn(b, _):
        columns_ref[b, :, 0:SUB] = jnp.transpose(q_ref[b])
        return 0

    lax.fori_loop(0, blocks, turn, 0, unroll=4)


def own_kernel(
    count_ref, pos_ref, vel_ref, rho_ref, mass_ref, out_ref, q_ref, acc_ref, columns_ref, behind_ref, *, rows, cols
):
    blocks = rows * cols
    lanes = q_ref.shape[2]
    flat = q_ref.reshape(blocks * SUB, lanes)

    def fill(g, _):
        here = pl.ds(pl.multiple_of(g * SUB, SUB), SUB)
        density = rho_ref[here, :]
        values = [
            pos_ref[0, here, :],
            pos_ref[1, here, :],
            vel_ref[0, here, :],
            vel_ref[1, here, :],
            density,
            pressure_ratio(density),
            mass_ref[here, :],
            density,
        ]
        for k in range(SUB):
            flat[pl.ds(g * SUB * SUB + k, SUB, stride=SUB), :] = values[k]
        return 0

    lax.fori_loop(0, blocks // SUB, fill, 0)

    def clear(b, _):
        acc_ref[b] = jnp.zeros((3, SUB, lanes), f32)
        return 0

    lax.fori_loop(0, blocks, clear, 0, unroll=4)
    behind_ref[...] = jnp.zeros(behind_ref.shape, f32)
    turn_columns(q_ref, columns_ref, blocks)

    def run(r, c, steps):
        center = r * cols + c
        near = [
            (center + sx * cols + sy, center + sx * cols + sy, float(sx), float(sy), (sx, sy) != (0, 0))
            for sx, sy in steps
        ]
        center_block(
            q_ref, columns_ref, behind_ref, acc_ref, out_ref, center, count_ref[center], near,
            jnp.maximum(center - 1, 0),
        )

    def one_row(r, _):
        run(r, 0, [(0, 1), (1, 0), (1, 1), (0, 0)])

        def middle(c, _):
            run(r, c, [(0, 1), (1, -1), (1, 0), (1, 1), (0, 0)])
            return 0

        lax.fori_loop(1, cols - 1, middle, 0)
        run(r, cols - 1, [(1, -1), (1, 0), (0, 0)])
        return 0

    lax.fori_loop(0, rows - 1, one_row, 0)

    def last_row(c, _):
        run(rows - 1, c, [(0, 1), (0, 0)])
        return 0

    lax.fori_loop(0, cols - 1, last_row, 0)
    run(rows - 1, cols - 1, [(0, 0)])
    out_ref[blocks - 1] = jnp.zeros((SUB, lanes), f32)
    sub = lax.broadcasted_iota(jnp.int32, (SUB, lanes), 0)

    def close(b, _):
        part = acc_ref[b]
        rows_sum = [jnp.sum(part[k], axis=0, keepdims=True) for k in range(3)]
        front = jnp.concatenate(rows_sum + [jnp.zeros((SUB - 3, lanes), f32)], axis=0)
        behind = out_ref[b]
        out_ref[b] = jnp.where(sub == 2, front + behind, front - behind)
        return 0

    lax.fori_loop(0, blocks, close, 0, unroll=4)


def halo_kernel(
    count_ref, index_ref, step_ref, halo_ref, q_ref, own_ref, wind_ref, out_ref, peak_ref, acc_ref, all_ref, columns_ref
):
    blocks, _, lanes = q_ref.shape
    edges = halo_ref.shape[0]
    all_ref[0:blocks] = q_ref[...]
    all_ref[blocks : blocks + edges] = halo_ref[...]

    def clear(b, _):
        acc_ref[b] = jnp.zeros((3, SUB, lanes), f32)
        return 0

    lax.fori_loop(0, blocks + 1, clear, 0)
    turn_columns(halo_ref, columns_ref, edges)

    def one_center(n, _):
        near = [
            (
                index_ref[6 * n + 2 * k],
                index_ref[6 * n + 2 * k + 1],
                step_ref[6 * n + 2 * k],
                step_ref[6 * n + 2 * k + 1],
                False,
            )
            for k in range(3)
        ]
        center_block(all_ref, columns_ref, None, acc_ref, None, n, count_ref[n], near, None)
        return 0

    lax.fori_loop(0, edges, one_center, 0)
    peak_ref[...] = jnp.zeros(peak_ref.shape, f32)

    def close(b, _):
        part = acc_ref[b]
        total = [jnp.sum(part[k], axis=0, keepdims=True) + own_ref[b, k : k + 1, :] for k in range(3)]
        mass = q_ref[b, 6:7, :]
        live = mass > 0.0
        scale = grad_coef / jnp.where(live, mass, 1.0)
        here = pl.ds(b, 1)
        acc_x = jnp.where(live, wind_ref[0, here, :] - scale * total[0], 0.0)
        acc_y = jnp.where(live, wind_ref[1, here, :] - scale * total[1], 0.0)
        out_ref[0, here, :] = acc_x
        out_ref[1, here, :] = acc_y
        out_ref[2, here, :] = jnp.where(live, scale * total[2], 0.0)
        peak_ref[0:1] = jnp.maximum(peak_ref[0:1], acc_x * acc_x + acc_y * acc_y)
        return 0

    lax.fori_loop(0, blocks, close, 0, unroll=4)


def halo_lists(rows, cols):
    index, step = [], []

    def add(r, c, steps):
        for sx, sy in steps:
            inside = 0 <= r + sx < rows and 0 <= c + sy < cols
            block = (r + sx) * cols + c + sy if inside else 0
            index.extend([block, block if inside else rows * cols])
            step.extend([sx, sy])

    for c in range(cols):
        add(-1, c, [(1, -1), (1, 0), (1, 1)])
    for c in range(cols):
        add(rows, c, [(-1, -1), (-1, 0), (-1, 1)])
    for r in range(-1, rows + 1):
        add(r, -1, [(-1, 1), (0, 1), (1, 1)])
    for r in range(-1, rows + 1):
        add(r, cols, [(-1, -1), (0, -1), (1, -1)])
    return np.asarray(index, np.int32), np.asarray(step, np.float32)


def spaces(smem, vmem):
    return [pl.BlockSpec(memory_space=pltpu.SMEM)] * smem + [pl.BlockSpec(memory_space=pltpu.VMEM)] * vmem


def own_forces(counts, positions, velocity, density, mass, rows, cols):
    blocks, lanes = density.shape
    shape = jax.ShapeDtypeStruct((blocks, SUB, lanes), f32)
    return pl.pallas_call(
        functools.partial(own_kernel, rows=rows, cols=cols),
        out_shape=(shape, shape),
        in_specs=spaces(1, 4),
        out_specs=tuple(spaces(0, 2)),
        scratch_shapes=[
            pltpu.VMEM((blocks, 3, SUB, lanes), f32),
            pltpu.VMEM((blocks, lanes, lanes), f32),
            pltpu.VMEM((3, lanes, lanes), f32),
        ],
        compiler_params=pltpu.CompilerParams(vmem_limit_bytes=VMEM_LIMIT),
        cost_estimate=pl.CostEstimate(flops=400_000_000, bytes_accessed=2_000_000, transcendentals=20_000_000),
    )(counts, positions, velocity, density, mass)


def halo_forces(counts, halo, fields, own, wind, rows, cols):
    blocks, _, lanes = fields.shape
    edges = halo.shape[0]
    index, step = halo_lists(rows, cols)
    return pl.pallas_call(
        halo_kernel,
        out_shape=(
            jax.ShapeDtypeStruct((3, blocks, lanes), f32),
            jax.ShapeDtypeStruct((SUB, lanes), f32),
        ),
        in_specs=spaces(3, 4),
        out_specs=tuple(spaces(0, 2)),
        scratch_shapes=[
            pltpu.VMEM((blocks + 1, 3, SUB, lanes), f32),
            pltpu.VMEM((blocks + edges, SUB, lanes), f32),
            pltpu.VMEM((edges, lanes, lanes), f32),
        ],
        compiler_params=pltpu.CompilerParams(vmem_limit_bytes=VMEM_LIMIT),
    )(counts, jnp.asarray(index), jnp.asarray(step), halo, fields, own, wind)


def pick_kernel(slot_ref, keep_ref, table_ref, out_ref):
    count, blocks, lanes = table_ref.shape
    for g in range(slot_ref.shape[0] // SUB):
        here = slice(g * SUB, g * SUB + SUB)
        slots = slot_ref[here]
        block_of = slots // lanes
        lane_of = slots % lanes

        def one(b, picked):
            hit = block_of == b
            rows = [jnp.broadcast_to(table_ref[k, pl.ds(b, 1), :], (SUB, lanes)) for k in range(count)]
            got = [jnp.take_along_axis(row, lane_of, axis=1, mode="promise_in_bounds") for row in rows]
            return tuple(jnp.where(hit, new, old) for new, old in zip(got, picked))

        start = (jnp.zeros((SUB, lanes), f32),) * count
        picked = lax.fori_loop(0, blocks, one, start, unroll=8)
        for k in range(count):
            out_ref[k, here] = picked[k] * keep_ref[here]


def pick(slots, keep, table, ways):
    count = table.shape[0]
    rows, lanes = slots.shape
    picked = pl.pallas_call(
        pick_kernel,
        out_shape=jax.ShapeDtypeStruct((count, rows, lanes), f32),
        in_specs=spaces(0, 3),
        out_specs=pl.BlockSpec(memory_space=pltpu.VMEM),
        compiler_params=pltpu.CompilerParams(vmem_limit_bytes=VMEM_LIMIT),
    )(slots, keep, table)
    return picked.reshape(count, ways, rows // ways, lanes)


def send_on(picked):
    return [
        passed_along(picked[:, 0], "shore", 1),
        passed_along(picked[:, 1], "shore", -1),
        passed_along(picked[:, 2], "cross", 1),
        passed_along(picked[:, 3], "cross", -1),
    ]


def time_step(peak_acc, peak_speed):
    return 0.25 * smooth / (sound_speed + peak_speed + jnp.sqrt(smooth * peak_acc))


def body(
    positions,
    velocity,
    density,
    particle_mass,
    cell_count,
    wind_seed,
    wind_table,
    migrant_slot,
    migrant_count,
):
    _, rows, cols, lanes = positions.shape
    blocks = rows * cols
    slot_ids = jnp.arange(lanes, dtype=jnp.int32)
    alive = slot_ids[None, None, :] < cell_count[:, :, None]
    live = alive.astype(f32)
    live_mass = particle_mass * live
    filled = jnp.broadcast_to(cell_count[:, :, None].astype(f32), live.shape)

    def rows_of(cut):
        there = density[cut]
        parts = [positions[0][cut], positions[1][cut], velocity[0][cut], velocity[1][cut]]
        parts += [there, pressure_ratio(there), live_mass[cut], filled[cut]]
        return jnp.stack(parts, axis=2)

    above = passed_along(rows_of(np.s_[rows - 1 :, :]), "shore", 1)
    below = passed_along(rows_of(np.s_[:1, :]), "shore", -1)
    west = rows_of(np.s_[:, :1])
    east = rows_of(np.s_[:, cols - 1 :])
    left = jnp.concatenate([above[:, cols - 1 :], east, below[:, cols - 1 :]], axis=0)
    right = jnp.concatenate([above[:, :1], west, below[:, :1]], axis=0)
    left, right, held_mass = lax.optimization_barrier((left, right, live_mass))
    left = passed_along(left, "cross", 1)
    right = passed_along(right, "cross", -1)
    halo = jnp.concatenate([z.reshape(-1, SUB, lanes) for z in (above, below, left, right)], axis=0)
    halo_count = halo[:, 7, 0].astype(jnp.int32)

    own, fields = own_forces(
        cell_count.reshape(-1),
        positions.reshape(2, blocks, lanes),
        velocity.reshape(2, blocks, lanes),
        density.reshape(blocks, lanes),
        held_mass.reshape(blocks, lanes),
        rows,
        cols,
    )

    level_ids = jnp.arange(wind_table.shape[1], dtype=jnp.int32)
    one_hot = (wind_seed[None] == level_ids[:, None, None, None]).astype(f32)
    windage = jnp.einsum("cl,lxyp->cxyp", wind_table, one_hot, precision=lax.Precision.HIGHEST)

    ways = migrant_slot.shape[2]
    width = migrant_slot.shape[3]
    slots = migrant_slot.reshape(-1, lanes)
    keep = jnp.arange(width, dtype=jnp.int32)[None, :] < migrant_count.reshape(ways, 1)
    keep = keep.astype(f32).reshape(-1, lanes)
    early = jnp.stack(
        [
            positions[0] * live,
            positions[1] * live,
            velocity[0] * live,
            velocity[1] * live,
            density * live,
            live_mass,
        ]
    )
    came_early = send_on(pick(slots, keep, early.reshape(-1, blocks, lanes), ways))

    late, peak = halo_forces(
        halo_count, halo, fields, own, windage.reshape(2, blocks, lanes), rows, cols
    )
    speed_sq = velocity[0] * velocity[0] + velocity[1] * velocity[1]
    highest = jnp.max(peak, axis=(0, 1), keepdims=True)
    fastest = jnp.max((speed_sq * live).reshape(blocks, lanes), axis=(0, 1), keepdims=True)
    first = lax.broadcasted_iota(jnp.int32, (1, lanes), 1) == 0
    peaks = jnp.sqrt(everywhere_max(jnp.where(first, highest, fastest)))
    delta_t = time_step(peaks[0, 0], peaks[0, 1])
    came_late = send_on(pick(slots, keep, late, ways))

    acceleration = late[:2].reshape(2, rows, cols, lanes)
    rate = late[2].reshape(rows, cols, lanes)
    new_velocity = (velocity + delta_t * acceleration) * live[None]
    new_position = (positions + delta_t * new_velocity) * live[None]
    new_density = (density + delta_t * rate) * live
    state_next = jnp.concatenate([new_position, new_velocity, new_density[None], acceleration])

    at = jnp.stack(came_early)
    on = jnp.stack(came_late)
    moved_velocity = at[:, 2:4] + delta_t * on[:, 0:2]
    moved_position = at[:, 0:2] + delta_t * moved_velocity
    moved_density = at[:, 4:5] + delta_t * on[:, 2:3]
    arrivals = jnp.concatenate(
        [moved_position, moved_velocity, moved_density, at[:, 5:6], on[:, 0:2]], axis=1
    )
    return (state_next, arrivals.reshape(1, 1, ways, arrivals.shape[1], width))


def solution(mesh):
    in_specs = (
        P(None, "shore", "cross", None),
        P(None, "shore", "cross", None),
        P("shore", "cross", None),
        P("shore", "cross", None),
        P("shore", "cross"),
        P("shore", "cross", None),
        P(),
        P("shore", "cross", None, None),
        P("shore", "cross", None),
    )
    out_specs = (P(None, "shore", "cross", None), P("shore", "cross", None, None, None))
    return jax.shard_map(body, mesh=mesh, in_specs=in_specs, out_specs=out_specs, check_vma=False)
```

time: 226 us -> 171 us (0.76)
  Pallas kernels: 142 us -> 103 us
  waiting for transfers between devices: 18.4 us -> 5.5 us
  other arithmetic: 15.2 us -> 7.62 us
  starting transfers between devices: 39 us -> 42.7 us
    pallas_call x1, Pallas kernels: 95.3 us -> 59.6 us  [own_forces(): pl.pallas_call(functools.partial(own_kernel, rows=rows, cols=cols), out_s...]
    ppermute x5, waiting for transfers between devices: 13.2 us -> 3.73 us  [everywhere_max(): array = jnp.maximum(array, lax.ppermute(array, axis, pairs))]
    unnamed x10 -> x7, other arithmetic: 4.68 us -> 0.15 us
    ppermute x12, starting transfers between devices: 34.6 us -> 38.3 us  [passed_along(): return lax.ppermute(array, axis, pairs)]
    ppermute x12, waiting for transfers between devices: 5.18 us -> 1.78 us  [passed_along(): return lax.ppermute(array, axis, pairs)]
    pallas_call x1, Pallas kernels: 22.5 us -> 19.1 us  [halo_forces(): pl.pallas_call(halo_kernel, out_shape=(jax.ShapeDtypeStruct((3, blocks, l...]
    reduce_sum x1 -> x0, other arithmetic: 3.28 us -> none  [body(): wide_count = jnp.sum(extended[:, 7] > 0.0, axis=1, dtype=jnp.int32)]
    unnamed x27 -> x42, local copies, waits for them, and re-layouts: 4.27 us -> 5.36 us
  transfers between devices with their start and end apart: 17 -> 17, of which waited for: 6 -> 3; matrix products, arithmetic and copies ran while one was open for 4% -> 3% of each run, Pallas kernels for 48% -> 49%
where the time goes in v2:
time: 171 us; the launch traced here: 170 us
  Pallas kernels  103 us (60%)
  starting transfers between devices  42.7 us (25%)
  local copies, waits for them, and re-layouts  8.57 us (5%)
  other arithmetic  7.62 us (4%)
  waiting for transfers between devices  5.5 us (3%)
  between operations  2.69 us (2%)
    pallas_call x1, Pallas kernels, own_forces(): pl.pallas_call(functools.partial(own_kernel, rows=rows, cols=cols), out_s...  59.6 us
    ppermute x12, starting transfers between devices, passed_along(): return lax.ppermute(array, axis, pairs)  38.3 us
    pallas_call x2, Pallas kernels, pick(): pl.pallas_call(pick_kernel, out_shape=jax.ShapeDtypeStruct((count, rows,...  24.2 us
    pallas_call x1, Pallas kernels, halo_forces(): pl.pallas_call(halo_kernel, out_shape=(jax.ShapeDtypeStruct((3, blocks, l...  19.1 us
    unnamed x42, local copies, waits for them, and re-layouts  5.36 us
    ppermute x5, starting transfers between devices, everywhere_max(): array = jnp.maximum(array, lax.ppermute(array, axis, pairs))  4.4 us
    ppermute x5, waiting for transfers between devices, everywhere_max(): array = jnp.maximum(array, lax.ppermute(array, axis, pairs))  3.73 us
  transfers between devices with their start and end apart: 17, of which 3 were waited for; matrix products, arithmetic and copies ran while one was open for 3% of the time, Pallas kernels for 49%

profile of v2, /device:TPU:6, one launch (start us, length us, event | category | flops | bytes accessed | tf_op | source)
XLA Modules:
  0.0 170.4 jit_solution(4914434511744790467)
XLA Ops:
  5.5 1.9 %collective-permute-start = (f32[1,8,8,128]{3,0,2,1:T(1,128)S(1)}, f32[1,8,8,128]{3,0,2,1:T(1,128)S(1)}, u32[]{:S(2)}, u32[]{:S(2)}) collective-permute-start(f32[1,8,8,128]{3,0,2,1:T(1,128)S(1)} %constant_dynamic-update-slice_fusion), channel_id=1, source_target_pairs={{0,8},{8,16},{16,24},{1,9},{9,17},{17,25},{2,10},{10,18},{18,26},{... | collective-permute-start | bytes 98312 | tf_op jit(solution)/shard_map/ppermute | solution.py:24
  7.5 3.6 %collective-permute-start.1 = (f32[1,8,8,128]{3,2,0,1:T(8,128)S(1)}, f32[1,8,8,128]{3,2,0,1:T(8,128)S(1)}, u32[]{:S(2)}, u32[]{:S(2)}) collective-permute-start(f32[1,8,8,128]{3,2,0,1:T(8,128)S(1)} %stack.176), channel_id=1, source_target_pairs={{8,0},{16,8},{24,16},{9,1},{17,9},{25,17},{10,2},{18,10},{26,18},{... | collective-permute-start | bytes 98312 | tf_op jit(solution)/shard_map/ppermute | solution.py:24
  13.5 3.4 %collective-permute-start.2 = (f32[18,1,8,128]{3,0,2,1:T(8,128)S(1)}, f32[18,1,8,128]{3,0,2,1:T(8,128)S(1)}, u32[]{:S(2)}, u32[]{:S(2)}) collective-permute-start(f32[18,1,8,128]{3,0,2,1:T(8,128)S(1)} %pad_maximum_fusion.3), channel_id=1, source_target_pairs={{0,1},{1,2},{2,3},{3,4},{4,5},{5,6},{6,7},{8,9},{9,10},{10,11},{11... | collective-permute-start | bytes 221192 | tf_op jit(solution)/shard_map/ppermute | solution.py:24
  16.9 2.4 %collective-permute-start.3 = (f32[18,1,8,128]{3,2,0,1:T(8,128)S(1)}, f32[18,1,8,128]{3,2,0,1:T(8,128)S(1)}, u32[]{:S(2)}, u32[]{:S(2)}) collective-permute-start(f32[18,1,8,128]{3,2,0,1:T(8,128)S(1)} %pad_maximum_fusion.5), channel_id=1, source_target_pairs={{1,0},{2,1},{3,2},{4,3},{5,4},{6,5},{7,6},{9,8},{10,9},{11,10},{12... | collective-permute-start | bytes 221192 | tf_op jit(solution)/shard_map/ppermute | solution.py:24
  20.3 13.5 %shard_map.124 = f32[6,56,128]{2,1,0:T(8,128)S(1)} custom-call(s32[56,128]{1,0:T(8,128)S(1)} %reshape.149.slot_ref, f32[56,128]{1,0:T(8,128)S(1)} %compare_convert_fusion.keep_ref, f32[6,128,128]{2,1,0:T(8,128)S(1)} %get-tuple-element.18.table_ref), custom_call_target="tpu_custom_call" | custom-call | tf_op jit(solution)/shard_map/pallas_call | solution.py:351
  33.8 59.6 %shard_map.122 = (f32[128,8,128]{2,1,0:T(8,128)S(1)}, f32[128,8,128]{2,1,0:T(8,128)S(1)}) custom-call(s32[128]{0:T(128)S(1)} %reshape.142.count_ref, f32[2,128,128]{2,1,0:T(8,128)S(1)} %bitcast.167, f32[2,128,128]{2,1,0:T(8,128)S(1)} %bitcast.168, f32[128,128]{1,0:T(8,128)S(1)} %bitcast.170, f32[128,128]{1,0:T(8,128)S(1)} %bitcast.171), custom_call_target="tpu_custom_call" | custom-call | flops 400000000 | bytes 2000000 | tf_op jit(solution)/shard_map/pallas_call | solution.py:292
  95.2 19.1 %shard_map.123 = (f32[3,128,128]{2,1,0:T(8,128)S(1)}, f32[8,128]{1,0:T(8,128)S(1)}) custom-call(s32[52]{0:T(128)S(1)} %fusion.10.count_ref, s32[312]{0:T(512)S(1)} %copy-done.4, f32[312]{0:T(512)S(1)} %copy-done.5, f32[52,8,128]{2,1,0:T(8,128)S(1)} %pad_maximum_fusion.1.halo_ref, f32[128,8,128]{2,1,0:T(8,128)S(1)} %get-tuple-element.12.q_ref, ...), custom_call_target="tpu_custom_call" | custom-call | tf_op jit(solution)/shard_map/pallas_call | solution.py:311
  114.9 1.3 compare_select_fusion
  116.3 1.9 %collective-permute-start.9 = (f32[6,14,128]{2,1,0:T(8,128)S(1)}, f32[6,14,128]{2,1,0:T(8,128)S(1)}, u32[]{:S(2)}, u32[]{:S(2)}) collective-permute-start(f32[6,14,128]{2,1,0:T(8,128)S(1)} %get-tuple-element.22), channel_id=1, source_target_pairs={{0,8},{8,16},{16,24},{1,9},{9,17},{17,25},{2,10},{10,18},{18,26},{... | collective-permute-start | bytes 129032 | tf_op jit(solution)/shard_map/ppermute | solution.py:24
  118.2 6.0 %collective-permute-start.10 = (f32[6,14,128]{2,1,0:T(8,128)S(1)}, f32[6,14,128]{2,1,0:T(8,128)S(1)}, u32[]{:S(2)}, u32[]{:S(2)}) collective-permute-start(f32[6,14,128]{2,1,0:T(8,128)S(1)} %get-tuple-element.23), channel_id=1, source_target_pairs={{8,0},{16,8},{24,16},{9,1},{17,9},{25,17},{10,2},{18,10},{26,18},{... | collective-permute-start | bytes 129032 | tf_op jit(solution)/shard_map/ppermute | solution.py:24
  124.2 4.7 %collective-permute-start.11 = (f32[6,14,128]{2,1,0:T(8,128)S(1)}, f32[6,14,128]{2,1,0:T(8,128)S(1)}, u32[]{:S(2)}, u32[]{:S(2)}) collective-permute-start(f32[6,14,128]{2,1,0:T(8,128)S(1)} %get-tuple-element.25), channel_id=1, source_target_pairs={{0,1},{1,2},{2,3},{3,4},{4,5},{5,6},{6,7},{8,9},{9,10},{10,11},{11... | collective-permute-start | bytes 129032 | tf_op jit(solution)/shard_map/ppermute | solution.py:24
  128.9 1.9 %collective-permute-start.12 = (f32[6,14,128]{2,1,0:T(8,128)S(1)}, f32[6,14,128]{2,1,0:T(8,128)S(1)}, u32[]{:S(2)}, u32[]{:S(2)}) collective-permute-start(f32[6,14,128]{2,1,0:T(8,128)S(1)} %get-tuple-element.24), channel_id=1, source_target_pairs={{1,0},{2,1},{3,2},{4,3},{5,4},{6,5},{7,6},{9,8},{10,9},{11,10},{12... | collective-permute-start | bytes 129032 | tf_op jit(solution)/shard_map/ppermute | solution.py:24
  130.8 1.3 fusion.41
  132.1 1.3 collective-permute-start.5
  133.5 2.2 %collective-permute-done.5 = f32[1,128]{1,0:T(1,128)S(1)} collective-permute-done((f32[1,128]{1,0:T(1,128)S(1)}, f32[1,128]{1,0:T(1,128)S(1)}, u32[]{:S(2)}, u32[]{:S(2)}) %collective-permute-start.5) | collective-permute-done | bytes 544 | tf_op jit(solution)/shard_map/ppermute | solution.py:36
  135.8 1.3 fusion.42
  137.1 3.0 %collective-permute-start.6 = (f32[1,128]{1,0:T(1,128)S(1)}, f32[1,128]{1,0:T(1,128)S(1)}, u32[]{:S(2)}, u32[]{:S(2)}) collective-permute-start(f32[1,128]{1,0:T(1,128)S(1)} %fusion.42), channel_id=1, source_target_pairs={{0,4},{1,5},{2,6},{3,7},{4,0},{5,1},{6,2},{7,3},{8,12},{9,13},{10,... | collective-permute-start | bytes 1544 | tf_op jit(solution)/shard_map/ppermute | solution.py:36
  140.1 1.5 collective-permute-done.6
  141.6 10.7 %shard_map.125 = f32[3,56,128]{2,1,0:T(8,128)S(1)} custom-call(s32[56,128]{1,0:T(8,128)S(1)} %reshape.149.slot_ref, f32[56,128]{1,0:T(8,128)S(1)} %compare_convert_fusion.keep_ref, f32[3,128,128]{2,1,0:T(8,128)S(1)} %get-tuple-element.15.table_ref), custom_call_target="tpu_custom_call" | custom-call | tf_op jit(solution)/shard_map/pallas_call | solution.py:351
  152.4 2.4 %collective-permute-start.13 = (f32[3,14,128]{2,1,0:T(8,128)S(1)}, f32[3,14,128]{2,1,0:T(8,128)S(1)}, u32[]{:S(2)}, u32[]{:S(2)}) collective-permute-start(f32[3,14,128]{2,1,0:T(8,128)S(1)} %get-tuple-element.38), channel_id=1, source_target_pairs={{0,8},{8,16},{16,24},{1,9},{9,17},{17,25},{2,10},{10,18},{18,26},{... | collective-permute-start | bytes 64520 | tf_op jit(solution)/shard_map/ppermute | solution.py:24
  154.8 3.2 %collective-permute-start.14 = (f32[3,14,128]{2,1,0:T(8,128)S(1)}, f32[3,14,128]{2,1,0:T(8,128)S(1)}, u32[]{:S(2)}, u32[]{:S(2)}) collective-permute-start(f32[3,14,128]{2,1,0:T(8,128)S(1)} %get-tuple-element.40), channel_id=1, source_target_pairs={{8,0},{16,8},{24,16},{9,1},{17,9},{25,17},{10,2},{18,10},{26,18},{... | collective-permute-start | bytes 64520 | tf_op jit(solution)/shard_map/ppermute | solution.py:24
  158.1 4.8 %collective-permute-start.15 = (f32[3,14,128]{2,1,0:T(8,128)S(1)}, f32[3,14,128]{2,1,0:T(8,128)S(1)}, u32[]{:S(2)}, u32[]{:S(2)}) collective-permute-start(f32[3,14,128]{2,1,0:T(8,128)S(1)} %get-tuple-element.39), channel_id=1, source_target_pairs={{0,1},{1,2},{2,3},{3,4},{4,5},{5,6},{6,7},{8,9},{9,10},{10,11},{11... | collective-permute-start | bytes 64520 | tf_op jit(solution)/shard_map/ppermute | solution.py:24
  162.9 1.9 %collective-permute-start.16 = (f32[3,14,128]{2,1,0:T(8,128)S(1)}, f32[3,14,128]{2,1,0:T(8,128)S(1)}, u32[]{:S(2)}, u32[]{:S(2)}) collective-permute-start(f32[3,14,128]{2,1,0:T(8,128)S(1)} %get-tuple-element.41), channel_id=1, source_target_pairs={{1,0},{2,1},{3,2},{4,3},{5,4},{6,5},{7,6},{9,8},{10,9},{11,10},{12... | collective-permute-start | bytes 64520 | tf_op jit(solution)/shard_map/ppermute | solution.py:24
  167.8 1.7 %collective-permute-done.16 = f32[3,14,128]{2,1,0:T(8,128)S(1)} collective-permute-done((f32[3,14,128]{2,1,0:T(8,128)S(1)}, f32[3,14,128]{2,1,0:T(8,128)S(1)}, u32[]{:S(2)}, u32[]{:S(2)}) %collective-permute-start.16) | collective-permute-done | bytes 21536 | tf_op jit(solution)/shard_map/ppermute | solution.py:24
  (120 shorter events, 12.9 us)
Async XLA Ops:
  0.6 10.9 %copy-start = (f32[2,16]{1,0:T(2,128)S(1)}, f32[2,16]{1,0:T(2,128)}, u32[]{:S(2)}) copy-start(f32[2,16]{1,0:T(2,128)} %param.17) | copy-start | bytes 388
  0.6 0.8 copy-start.7
  1.5 1.0 copy-start.1
  1.5 1.0 copy-start.2
  3.2 0.8 copy-start.3
  4.2 0.8 copy-start.6
  5.5 8.0 %collective-permute-start = (f32[1,8,8,128]{3,0,2,1:T(1,128)S(1)}, f32[1,8,8,128]{3,0,2,1:T(1,128)S(1)}, u32[]{:S(2)}, u32[]{:S(2)}) collective-permute-start(f32[1,8,8,128]{3,0,2,1:T(1,128)S(1)} %constant_dynamic-update-slice_fusion), channel_id=1, source_target_pairs={{0,8},{8,16},{16,24},{1,9},{9,17},{17,25},{2,10},{10,18},{18,26},{... | collective-permute-start | bytes 98312 | tf_op jit(solution)/shard_map/ppermute | solution.py:24
  7.5 5.9 %collective-permute-start.1 = (f32[1,8,8,128]{3,2,0,1:T(8,128)S(1)}, f32[1,8,8,128]{3,2,0,1:T(8,128)S(1)}, u32[]{:S(2)}, u32[]{:S(2)}) collective-permute-start(f32[1,8,8,128]{3,2,0,1:T(8,128)S(1)} %stack.176), channel_id=1, source_target_pairs={{8,0},{16,8},{24,16},{9,1},{17,9},{25,17},{10,2},{18,10},{26,18},{... | collective-permute-start | bytes 98312 | tf_op jit(solution)/shard_map/ppermute | solution.py:24
  11.3 0.8 copy-start.10
  13.5 79.9 %collective-permute-start.2 = (f32[18,1,8,128]{3,0,2,1:T(8,128)S(1)}, f32[18,1,8,128]{3,0,2,1:T(8,128)S(1)}, u32[]{:S(2)}, u32[]{:S(2)}) collective-permute-start(f32[18,1,8,128]{3,0,2,1:T(8,128)S(1)} %pad_maximum_fusion.3), channel_id=1, source_target_pairs={{0,1},{1,2},{2,3},{3,4},{4,5},{5,6},{6,7},{8,9},{9,10},{10,11},{11... | collective-permute-start | bytes 221192 | tf_op jit(solution)/shard_map/ppermute | solution.py:24
  16.9 76.5 %collective-permute-start.3 = (f32[18,1,8,128]{3,2,0,1:T(8,128)S(1)}, f32[18,1,8,128]{3,2,0,1:T(8,128)S(1)}, u32[]{:S(2)}, u32[]{:S(2)}) collective-permute-start(f32[18,1,8,128]{3,2,0,1:T(8,128)S(1)} %pad_maximum_fusion.5), channel_id=1, source_target_pairs={{1,0},{2,1},{3,2},{4,3},{5,4},{6,5},{7,6},{9,8},{10,9},{11,10},{12... | collective-permute-start | bytes 221192 | tf_op jit(solution)/shard_map/ppermute | solution.py:24
  116.2 14.6 %collective-permute-start.4 = (f32[1,128]{1,0:T(1,128)S(1)}, f32[1,128]{1,0:T(1,128)S(1)}, u32[]{:S(2)}, u32[]{:S(2)}) collective-permute-start(f32[1,128]{1,0:T(1,128)S(1)} %compare_select_fusion), channel_id=1, source_target_pairs={{0,1},{1,0},{2,3},{3,2},{4,5},{5,4},{6,7},{7,6},{8,9},{9,8},{10,11... | collective-permute-start | bytes 1544 | tf_op jit(solution)/shard_map/ppermute | solution.py:36
  116.3 23.7 %collective-permute-start.9 = (f32[6,14,128]{2,1,0:T(8,128)S(1)}, f32[6,14,128]{2,1,0:T(8,128)S(1)}, u32[]{:S(2)}, u32[]{:S(2)}) collective-permute-start(f32[6,14,128]{2,1,0:T(8,128)S(1)} %get-tuple-element.22), channel_id=1, source_target_pairs={{0,8},{8,16},{16,24},{1,9},{9,17},{17,25},{2,10},{10,18},{18,26},{... | collective-permute-start | bytes 129032 | tf_op jit(solution)/shard_map/ppermute | solution.py:24
  118.2 21.8 %collective-permute-start.10 = (f32[6,14,128]{2,1,0:T(8,128)S(1)}, f32[6,14,128]{2,1,0:T(8,128)S(1)}, u32[]{:S(2)}, u32[]{:S(2)}) collective-permute-start(f32[6,14,128]{2,1,0:T(8,128)S(1)} %get-tuple-element.23), channel_id=1, source_target_pairs={{8,0},{16,8},{24,16},{9,1},{17,9},{25,17},{10,2},{18,10},{26,18},{... | collective-permute-start | bytes 129032 | tf_op jit(solution)/shard_map/ppermute | solution.py:24
  124.2 15.8 %collective-permute-start.11 = (f32[6,14,128]{2,1,0:T(8,128)S(1)}, f32[6,14,128]{2,1,0:T(8,128)S(1)}, u32[]{:S(2)}, u32[]{:S(2)}) collective-permute-start(f32[6,14,128]{2,1,0:T(8,128)S(1)} %get-tuple-element.25), channel_id=1, source_target_pairs={{0,1},{1,2},{2,3},{3,4},{4,5},{5,6},{6,7},{8,9},{9,10},{10,11},{11... | collective-permute-start | bytes 129032 | tf_op jit(solution)/shard_map/ppermute | solution.py:24
  128.9 11.2 %collective-permute-start.12 = (f32[6,14,128]{2,1,0:T(8,128)S(1)}, f32[6,14,128]{2,1,0:T(8,128)S(1)}, u32[]{:S(2)}, u32[]{:S(2)}) collective-permute-start(f32[6,14,128]{2,1,0:T(8,128)S(1)} %get-tuple-element.24), channel_id=1, source_target_pairs={{1,0},{2,1},{3,2},{4,3},{5,4},{6,5},{7,6},{9,8},{10,9},{11,10},{12... | collective-permute-start | bytes 129032 | tf_op jit(solution)/shard_map/ppermute | solution.py:24
  132.1 3.6 %collective-permute-start.5 = (f32[1,128]{1,0:T(1,128)S(1)}, f32[1,128]{1,0:T(1,128)S(1)}, u32[]{:S(2)}, u32[]{:S(2)}) collective-permute-start(f32[1,128]{1,0:T(1,128)S(1)} %fusion.41), channel_id=1, source_target_pairs={{0,2},{1,3},{2,0},{3,1},{4,6},{5,7},{6,4},{7,5},{8,10},{9,11},{10,... | collective-permute-start | bytes 1544 | tf_op jit(solution)/shard_map/ppermute | solution.py:36
  137.1 4.5 %collective-permute-start.6 = (f32[1,128]{1,0:T(1,128)S(1)}, f32[1,128]{1,0:T(1,128)S(1)}, u32[]{:S(2)}, u32[]{:S(2)}) collective-permute-start(f32[1,128]{1,0:T(1,128)S(1)} %fusion.42), channel_id=1, source_target_pairs={{0,4},{1,5},{2,6},{3,7},{4,0},{5,1},{6,2},{7,3},{8,12},{9,13},{10,... | collective-permute-start | bytes 1544 | tf_op jit(solution)/shard_map/ppermute | solution.py:36
  141.6 10.7 %collective-permute-start.7 = (f32[1,128]{1,0:T(1,128)S(1)}, f32[1,128]{1,0:T(1,128)S(1)}, u32[]{:S(2)}, u32[]{:S(2)}) collective-permute-start(f32[1,128]{1,0:T(1,128)S(1)} %max.17), channel_id=1, source_target_pairs={{0,8},{8,0},{16,24},{24,16},{1,9},{9,1},{17,25},{25,17},{2,10},{10... | collective-permute-start | bytes 1544 | tf_op jit(solution)/shard_map/ppermute | solution.py:36
  152.3 12.5 %collective-permute-start.8 = (f32[1,128]{1,0:T(1,128)S(1)}, f32[1,128]{1,0:T(1,128)S(1)}, u32[]{:S(2)}, u32[]{:S(2)}) collective-permute-start(f32[1,128]{1,0:T(1,128)S(1)} %max.18), channel_id=1, source_target_pairs={{0,16},{8,24},{16,0},{24,8},{1,17},{9,25},{17,1},{25,9},{2,18},{10... | collective-permute-start | bytes 1544 | tf_op jit(solution)/shard_map/ppermute | solution.py:36
  152.4 15.4 %collective-permute-start.13 = (f32[3,14,128]{2,1,0:T(8,128)S(1)}, f32[3,14,128]{2,1,0:T(8,128)S(1)}, u32[]{:S(2)}, u32[]{:S(2)}) collective-permute-start(f32[3,14,128]{2,1,0:T(8,128)S(1)} %get-tuple-element.38), channel_id=1, source_target_pairs={{0,8},{8,16},{16,24},{1,9},{9,17},{17,25},{2,10},{10,18},{18,26},{... | collective-permute-start | bytes 64520 | tf_op jit(solution)/shard_map/ppermute | solution.py:24
  154.8 12.9 %collective-permute-start.14 = (f32[3,14,128]{2,1,0:T(8,128)S(1)}, f32[3,14,128]{2,1,0:T(8,128)S(1)}, u32[]{:S(2)}, u32[]{:S(2)}) collective-permute-start(f32[3,14,128]{2,1,0:T(8,128)S(1)} %get-tuple-element.40), channel_id=1, source_target_pairs={{8,0},{16,8},{24,16},{9,1},{17,9},{25,17},{10,2},{18,10},{26,18},{... | collective-permute-start | bytes 64520 | tf_op jit(solution)/shard_map/ppermute | solution.py:24
  158.1 9.7 %collective-permute-start.15 = (f32[3,14,128]{2,1,0:T(8,128)S(1)}, f32[3,14,128]{2,1,0:T(8,128)S(1)}, u32[]{:S(2)}, u32[]{:S(2)}) collective-permute-start(f32[3,14,128]{2,1,0:T(8,128)S(1)} %get-tuple-element.39), channel_id=1, source_target_pairs={{0,1},{1,2},{2,3},{3,4},{4,5},{5,6},{6,7},{8,9},{9,10},{10,11},{11... | collective-permute-start | bytes 64520 | tf_op jit(solution)/shard_map/ppermute | solution.py:24
  162.9 6.6 %collective-permute-start.16 = (f32[3,14,128]{2,1,0:T(8,128)S(1)}, f32[3,14,128]{2,1,0:T(8,128)S(1)}, u32[]{:S(2)}, u32[]{:S(2)}) collective-permute-start(f32[3,14,128]{2,1,0:T(8,128)S(1)} %get-tuple-element.41), channel_id=1, source_target_pairs={{1,0},{2,1},{3,2},{4,3},{5,4},{6,5},{7,6},{9,8},{10,9},{11,10},{12... | collective-permute-start | bytes 64520 | tf_op jit(solution)/shard_map/ppermute | solution.py:24
  (4 other events, 2.8 us)

commit v3 on v2

--- a/solution.py
+++ b/solution.py
@@ -241,12 +241,12 @@
         return 0
 
     lax.fori_loop(0, edges, one_center, 0)
-    peak_ref[...] = jnp.zeros(peak_ref.shape, f32)
-
-    def close(b, _):
+    nothing = jnp.zeros((1, lanes), f32)
+
+    def close(b, peaks):
         part = acc_ref[b]
         total = [jnp.sum(part[k], axis=0, keepdims=True) + own_ref[b, k : k + 1, :] for k in range(3)]
-        mass = q_ref[b, 6:7, :]
+        speed_x, speed_y, mass = (q_ref[b, k : k + 1, :] for k in (2, 3, 6))
         live = mass > 0.0
         scale = grad_coef / jnp.where(live, mass, 1.0)
         here = pl.ds(b, 1)
@@ -255,10 +255,14 @@
         out_ref[0, here, :] = acc_x
         out_ref[1, here, :] = acc_y
         out_ref[2, here, :] = jnp.where(live, scale * total[2], 0.0)
-        peak_ref[0:1] = jnp.maximum(peak_ref[0:1], acc_x * acc_x + acc_y * acc_y)
-        return 0
-
-    lax.fori_loop(0, blocks, close, 0, unroll=4)
+        speed = jnp.where(live, speed_x * speed_x + speed_y * speed_y, 0.0)
+        return jnp.maximum(peaks[0], acc_x * acc_x + acc_y * acc_y), jnp.maximum(peaks[1], speed)
+
+    highest, fastest = lax.fori_loop(0, blocks, close, (nothing, nothing), unroll=4)
+    highest = jnp.max(highest, axis=1, keepdims=True)
+    fastest = jnp.max(fastest, axis=1, keepdims=True)
+    first = lax.broadcasted_iota(jnp.int32, peak_ref.shape, 1) == 0
+    peak_ref[...] = jnp.where(first, highest, fastest)
 
 
 def halo_lists(rows, cols):
@@ -327,22 +331,32 @@
 
 def pick_kernel(slot_ref, keep_ref, table_ref, out_ref):
     count, blocks, lanes = table_ref.shape
-    for g in range(slot_ref.shape[0] // SUB):
-        here = slice(g * SUB, g * SUB + SUB)
-        slots = slot_ref[here]
-        block_of = slots // lanes
-        lane_of = slots % lanes
-
-        def one(b, picked):
-            hit = block_of == b
-            rows = [jnp.broadcast_to(table_ref[k, pl.ds(b, 1), :], (SUB, lanes)) for k in range(count)]
-            got = [jnp.take_along_axis(row, lane_of, axis=1, mode="promise_in_bounds") for row in rows]
-            return tuple(jnp.where(hit, new, old) for new, old in zip(got, picked))
-
-        start = (jnp.zeros((SUB, lanes), f32),) * count
-        picked = lax.fori_loop(0, blocks, one, start, unroll=8)
+    sub = lax.broadcasted_iota(jnp.int32, (SUB, lanes), 0)
+
+    def group(g, _):
+        here = pl.ds(pl.multiple_of(g * SUB, SUB), SUB)
+        slots = slot_ref[here, :]
+        keep = keep_ref[here, :]
+        outs = [jnp.zeros((SUB, lanes), f32)] * count
+        for r in range(SUB):
+            wanted = jnp.broadcast_to(slots[r : r + 1], (SUB, lanes))
+            lane_of = wanted % lanes
+            offset = wanted // lanes - sub
+            picked = [jnp.zeros((SUB, lanes), f32)] * count
+            for t in range(0, blocks, SUB):
+                hit = offset == t
+                for k in range(count):
+                    got = jnp.take_along_axis(
+                        table_ref[k, t : t + SUB, :], lane_of, axis=1, mode="promise_in_bounds"
+                    )
+                    picked[k] = jnp.where(hit, got, picked[k])
+            for k in range(count):
+                outs[k] = jnp.where(sub == r, jnp.sum(picked[k], axis=0, keepdims=True), outs[k])
         for k in range(count):
-            out_ref[k, here] = picked[k] * keep_ref[here]
+            out_ref[k, here, :] = outs[k] * keep
+        return 0
+
+    lax.fori_loop(0, slot_ref.shape[0] // SUB, group, 0)
 
 
 def pick(slots, keep, table, ways):
@@ -437,18 +451,15 @@
             live_mass,
         ]
     )
-    came_early = send_on(pick(slots, keep, early.reshape(-1, blocks, lanes), ways))
+    still = pick(slots, keep, early.reshape(-1, blocks, lanes), ways)
 
     late, peak = halo_forces(
         halo_count, halo, fields, own, windage.reshape(2, blocks, lanes), rows, cols
     )
-    speed_sq = velocity[0] * velocity[0] + velocity[1] * velocity[1]
-    highest = jnp.max(peak, axis=(0, 1), keepdims=True)
-    fastest = jnp.max((speed_sq * live).reshape(blocks, lanes), axis=(0, 1), keepdims=True)
-    first = lax.broadcasted_iota(jnp.int32, (1, lanes), 1) == 0
-    peaks = jnp.sqrt(everywhere_max(jnp.where(first, highest, fastest)))
+    peaks = jnp.sqrt(everywhere_max(peak))
     delta_t = time_step(peaks[0, 0], peaks[0, 1])
-    came_late = send_on(pick(slots, keep, late, ways))
+    moving = pick(slots, keep, late, ways)
+    came = jnp.stack(send_on(jnp.concatenate([still, moving])))
 
     acceleration = late[:2].reshape(2, rows, cols, lanes)
     rate = late[2].reshape(rows, cols, lanes)
@@ -457,13 +468,11 @@
     new_density = (density + delta_t * rate) * live
     state_next = jnp.concatenate([new_position, new_velocity, new_density[None], acceleration])
 
-    at = jnp.stack(came_early)
-    on = jnp.stack(came_late)
-    moved_velocity = at[:, 2:4] + delta_t * on[:, 0:2]
-    moved_position = at[:, 0:2] + delta_t * moved_velocity
-    moved_density = at[:, 4:5] + delta_t * on[:, 2:3]
+    moved_velocity = came[:, 2:4] + delta_t * came[:, 6:8]
+    moved_position = came[:, 0:2] + delta_t * moved_velocity
+    moved_density = came[:, 4:5] + delta_t * came[:, 8:9]
     arrivals = jnp.concatenate(
-        [moved_position, moved_velocity, moved_density, at[:, 5:6], on[:, 0:2]], axis=1
+        [moved_position, moved_velocity, moved_density, came[:, 5:6], came[:, 6:8]], axis=1
     )
     return (state_next, arrivals.reshape(1, 1, ways, arrivals.shape[1], width))
 

time: 171 us -> 139 us (0.81)
  starting transfers between devices: 42.7 us -> 28.9 us
  Pallas kernels: 103 us -> 89.2 us
  other arithmetic: 7.62 us -> 2.62 us
    ppermute x12 -> x8, starting transfers between devices: 38.3 us -> 22.8 us  [passed_along(): return lax.ppermute(array, axis, pairs)]
    pallas_call x2, Pallas kernels: 24.2 us -> 10.1 us  [pick(): pl.pallas_call(pick_kernel, out_shape=jax.ShapeDtypeStruct((count, rows,...]
    max x4, other arithmetic: 2.6 us -> 0.02 us  [everywhere_max(): array = jnp.maximum(array, lax.ppermute(array, axis, pairs))]
    ppermute x5, starting transfers between devices: 4.4 us -> 6.14 us  [everywhere_max(): array = jnp.maximum(array, lax.ppermute(array, axis, pairs))]
    unnamed x42 -> x43, local copies, waits for them, and re-layouts: 5.36 us -> 5.36 us
  transfers between devices with their start and end apart: 17 -> 13, of which waited for: 3 -> 3; matrix products, arithmetic and copies ran while one was open for 3% -> 2% of each run, Pallas kernels for 49% -> 51%
where the time goes in v3:
time: 139 us; the launch traced here: 137 us
  Pallas kernels  89.2 us (64%)
  starting transfers between devices  28.9 us (21%)
  local copies, waits for them, and re-layouts  8.57 us (6%)
  waiting for transfers between devices  4.79 us (3%)
  between operations  2.65 us (2%)
  other arithmetic  2.62 us (2%)
    pallas_call x1, Pallas kernels, own_forces(): pl.pallas_call(functools.partial(own_kernel, rows=rows, cols=cols), out_s...  60.5 us
    ppermute x8, starting transfers between devices, passed_along(): return lax.ppermute(array, axis, pairs)  22.8 us
    pallas_call x1, Pallas kernels, halo_forces(): pl.pallas_call(halo_kernel, out_shape=(jax.ShapeDtypeStruct((3, blocks, l...  18.6 us
    pallas_call x2, Pallas kernels, pick(): pl.pallas_call(pick_kernel, out_shape=jax.ShapeDtypeStruct((count, rows,...  10.1 us
    ppermute x5, starting transfers between devices, everywhere_max(): array = jnp.maximum(array, lax.ppermute(array, axis, pairs))  6.14 us
    unnamed x43, local copies, waits for them, and re-layouts  5.36 us
    ppermute x5, waiting for transfers between devices, everywhere_max(): array = jnp.maximum(array, lax.ppermute(array, axis, pairs))  3.84 us
  transfers between devices with their start and end apart: 13, of which 3 were waited for; matrix products, arithmetic and copies ran while one was open for 2% of the time, Pallas kernels for 51%

profile of v3, /device:TPU:6, one launch (start us, length us, event | category | flops | bytes accessed | tf_op | source)
XLA Modules:
  0.0 137.2 jit_solution(2555606697518851731)
XLA Ops:
  0.7 0.8 copy.37
  1.5 0.9 fusion.36
  2.7 0.8 copy-done.3
  3.8 0.7 copy-done.7
  5.0 1.9 %collective-permute-start = (f32[1,8,8,128]{3,0,2,1:T(1,128)S(1)}, f32[1,8,8,128]{3,0,2,1:T(1,128)S(1)}, u32[]{:S(2)}, u32[]{:S(2)}) collective-permute-start(f32[1,8,8,128]{3,0,2,1:T(1,128)S(1)} %constant_dynamic-update-slice_fusion), channel_id=1, source_target_pairs={{0,8},{8,16},{16,24},{1,9},{9,17},{17,25},{2,10},{10,18},{18,26},{... | collective-permute-start | bytes 98312 | tf_op jit(solution)/shard_map/ppermute | solution.py:24
  7.0 3.6 %collective-permute-start.1 = (f32[1,8,8,128]{3,2,0,1:T(8,128)S(1)}, f32[1,8,8,128]{3,2,0,1:T(8,128)S(1)}, u32[]{:S(2)}, u32[]{:S(2)}) collective-permute-start(f32[1,8,8,128]{3,2,0,1:T(8,128)S(1)} %stack.161), channel_id=1, source_target_pairs={{8,0},{16,8},{24,16},{9,1},{17,9},{25,17},{10,2},{18,10},{26,18},{... | collective-permute-start | bytes 98312 | tf_op jit(solution)/shard_map/ppermute | solution.py:24
  12.3 3.4 %collective-permute-start.2 = (f32[18,1,8,128]{3,0,2,1:T(8,128)S(1)}, f32[18,1,8,128]{3,0,2,1:T(8,128)S(1)}, u32[]{:S(2)}, u32[]{:S(2)}) collective-permute-start(f32[18,1,8,128]{3,0,2,1:T(8,128)S(1)} %pad_maximum_fusion.4), channel_id=1, source_target_pairs={{0,1},{1,2},{2,3},{3,4},{4,5},{5,6},{6,7},{8,9},{9,10},{10,11},{11... | collective-permute-start | bytes 221192 | tf_op jit(solution)/shard_map/ppermute | solution.py:24
  15.7 2.4 %collective-permute-start.3 = (f32[18,1,8,128]{3,2,0,1:T(8,128)S(1)}, f32[18,1,8,128]{3,2,0,1:T(8,128)S(1)}, u32[]{:S(2)}, u32[]{:S(2)}) collective-permute-start(f32[18,1,8,128]{3,2,0,1:T(8,128)S(1)} %pad_maximum_fusion.5), channel_id=1, source_target_pairs={{1,0},{2,1},{3,2},{4,3},{5,4},{6,5},{7,6},{9,8},{10,9},{11,10},{12... | collective-permute-start | bytes 221192 | tf_op jit(solution)/shard_map/ppermute | solution.py:24
  19.1 60.5 %shard_map.122 = (f32[128,8,128]{2,1,0:T(8,128)S(1)}, f32[128,8,128]{2,1,0:T(8,128)S(1)}) custom-call(s32[128]{0:T(128)S(1)} %reshape.112.count_ref, f32[2,128,128]{2,1,0:T(8,128)S(1)} %bitcast.147, f32[2,128,128]{2,1,0:T(8,128)S(1)} %bitcast.148, f32[128,128]{1,0:T(8,128)S(1)} %bitcast.150, f32[128,128]{1,0:T(8,128)S(1)} %bitcast.151), custom_call_target="tpu_custom_call" | custom-call | flops 400000000 | bytes 2000000 | tf_op jit(solution)/shard_map/pallas_call | solution.py:296
  79.7 1.0 fusion.11.count_ref
  81.4 18.6 %shard_map.123 = (f32[3,128,128]{2,1,0:T(8,128)S(1)}, f32[8,128]{1,0:T(8,128)S(1)}) custom-call(s32[52]{0:T(128)S(1)} %fusion.11.count_ref, s32[312]{0:T(512)S(1)} %copy-done.4, f32[312]{0:T(512)S(1)} %copy-done.5, f32[52,8,128]{2,1,0:T(8,128)S(1)} %pad_maximum_fusion.3.halo_ref, f32[128,8,128]{2,1,0:T(8,128)S(1)} %get-tuple-element.12.q_ref, ...), custom_call_target="tpu_custom_call" | custom-call | tf_op jit(solution)/shard_map/pallas_call | solution.py:315
  100.8 6.5 %shard_map.124 = f32[6,56,128]{2,1,0:T(8,128)S(1)} custom-call(s32[56,128]{1,0:T(8,128)S(1)} %reshape.119.slot_ref, f32[56,128]{1,0:T(8,128)S(1)} %compare_convert_fusion.keep_ref, f32[6,128,128]{2,1,0:T(8,128)S(1)} %get-tuple-element.20.table_ref), custom_call_target="tpu_custom_call" | custom-call | tf_op jit(solution)/shard_map/pallas_call | solution.py:365
  107.4 2.8 %collective-permute-start.5 = (f32[8,128]{1,0:T(8,128)S(1)}, f32[8,128]{1,0:T(8,128)S(1)}, u32[]{:S(2)}, u32[]{:S(2)}) collective-permute-start(f32[8,128]{1,0:T(8,128)S(1)} %max.15), channel_id=1, source_target_pairs={{0,2},{1,3},{2,0},{3,1},{4,6},{5,7},{6,4},{7,5},{8,10},{9,11},{10,... | collective-permute-start | bytes 12296 | tf_op jit(solution)/shard_map/ppermute | solution.py:36
  110.2 3.6 %shard_map.125 = f32[3,56,128]{2,1,0:T(8,128)S(1)} custom-call(s32[56,128]{1,0:T(8,128)S(1)} %reshape.119.slot_ref, f32[56,128]{1,0:T(8,128)S(1)} %compare_convert_fusion.keep_ref, f32[3,128,128]{2,1,0:T(8,128)S(1)} %get-tuple-element.15.table_ref), custom_call_target="tpu_custom_call" | custom-call | tf_op jit(solution)/shard_map/pallas_call | solution.py:365
  113.9 1.9 %collective-permute-start.6 = (f32[8,128]{1,0:T(8,128)S(1)}, f32[8,128]{1,0:T(8,128)S(1)}, u32[]{:S(2)}, u32[]{:S(2)}) collective-permute-start(f32[8,128]{1,0:T(8,128)S(1)} %max.16), channel_id=1, source_target_pairs={{0,4},{1,5},{2,6},{3,7},{4,0},{5,1},{6,2},{7,3},{8,12},{9,13},{10,... | collective-permute-start | bytes 12296 | tf_op jit(solution)/shard_map/ppermute | solution.py:36
  115.7 2.7 %collective-permute-done.6 = f32[8,128]{1,0:T(8,128)S(1)} collective-permute-done((f32[8,128]{1,0:T(8,128)S(1)}, f32[8,128]{1,0:T(8,128)S(1)}, u32[]{:S(2)}, u32[]{:S(2)}) %collective-permute-start.6) | collective-permute-done | bytes 4128 | tf_op jit(solution)/shard_map/ppermute | solution.py:36
  118.5 1.1 collective-permute-done.7
  119.6 1.4 %collective-permute-start.8 = (f32[8,128]{1,0:T(8,128)S(1)}, f32[8,128]{1,0:T(8,128)S(1)}, u32[]{:S(2)}, u32[]{:S(2)}) collective-permute-start(f32[8,128]{1,0:T(8,128)S(1)} %max.18), channel_id=1, source_target_pairs={{0,16},{8,24},{16,0},{24,8},{1,17},{9,25},{17,1},{25,9},{2,18},{10... | collective-permute-start | bytes 12296 | tf_op jit(solution)/shard_map/ppermute | solution.py:36
  121.0 2.0 %collective-permute-start.9 = (f32[9,14,128]{2,1,0:T(8,128)S(1)}, f32[9,14,128]{2,1,0:T(8,128)S(1)}, u32[]{:S(2)}, u32[]{:S(2)}) collective-permute-start(f32[9,14,128]{2,1,0:T(8,128)S(1)} %get-tuple-element.24), channel_id=1, source_target_pairs={{0,8},{8,16},{16,24},{1,9},{9,17},{17,25},{2,10},{10,18},{18,26},{... | collective-permute-start | bytes 193544 | tf_op jit(solution)/shard_map/ppermute | solution.py:24
  123.0 3.6 %collective-permute-start.10 = (f32[9,14,128]{2,1,0:T(8,128)S(1)}, f32[9,14,128]{2,1,0:T(8,128)S(1)}, u32[]{:S(2)}, u32[]{:S(2)}) collective-permute-start(f32[9,14,128]{2,1,0:T(8,128)S(1)} %get-tuple-element.25), channel_id=1, source_target_pairs={{8,0},{16,8},{24,16},{9,1},{17,9},{25,17},{10,2},{18,10},{26,18},{... | collective-permute-start | bytes 193544 | tf_op jit(solution)/shard_map/ppermute | solution.py:24
  126.6 2.6 %collective-permute-start.11 = (f32[9,14,128]{2,1,0:T(8,128)S(1)}, f32[9,14,128]{2,1,0:T(8,128)S(1)}, u32[]{:S(2)}, u32[]{:S(2)}) collective-permute-start(f32[9,14,128]{2,1,0:T(8,128)S(1)} %get-tuple-element.27), channel_id=1, source_target_pairs={{0,1},{1,2},{2,3},{3,4},{4,5},{5,6},{6,7},{8,9},{9,10},{10,11},{11... | collective-permute-start | bytes 193544 | tf_op jit(solution)/shard_map/ppermute | solution.py:24
  129.2 3.3 %collective-permute-start.12 = (f32[9,14,128]{2,1,0:T(8,128)S(1)}, f32[9,14,128]{2,1,0:T(8,128)S(1)}, u32[]{:S(2)}, u32[]{:S(2)}) collective-permute-start(f32[9,14,128]{2,1,0:T(8,128)S(1)} %get-tuple-element.26), channel_id=1, source_target_pairs={{1,0},{2,1},{3,2},{4,3},{5,4},{6,5},{7,6},{9,8},{10,9},{11,10},{12... | collective-permute-start | bytes 193544 | tf_op jit(solution)/shard_map/ppermute | solution.py:24
  134.6 0.8 pad_maximum_fusion
  135.4 0.9 collective-permute-done.12
  (110 shorter events, 6.5 us)
Async XLA Ops:
  0.6 10.4 %copy-start = (f32[2,16]{1,0:T(2,128)S(1)}, f32[2,16]{1,0:T(2,128)}, u32[]{:S(2)}) copy-start(f32[2,16]{1,0:T(2,128)} %param.17) | copy-start | bytes 388
  0.6 0.8 copy-start.6
  1.5 1.0 copy-start.1
  1.5 1.0 copy-start.2
  2.6 0.8 copy-start.3
  3.7 0.8 copy-start.7
  5.0 7.3 %collective-permute-start = (f32[1,8,8,128]{3,0,2,1:T(1,128)S(1)}, f32[1,8,8,128]{3,0,2,1:T(1,128)S(1)}, u32[]{:S(2)}, u32[]{:S(2)}) collective-permute-start(f32[1,8,8,128]{3,0,2,1:T(1,128)S(1)} %constant_dynamic-update-slice_fusion), channel_id=1, source_target_pairs={{0,8},{8,16},{16,24},{1,9},{9,17},{17,25},{2,10},{10,18},{18,26},{... | collective-permute-start | bytes 98312 | tf_op jit(solution)/shard_map/ppermute | solution.py:24
  7.0 5.2 %collective-permute-start.1 = (f32[1,8,8,128]{3,2,0,1:T(8,128)S(1)}, f32[1,8,8,128]{3,2,0,1:T(8,128)S(1)}, u32[]{:S(2)}, u32[]{:S(2)}) collective-permute-start(f32[1,8,8,128]{3,2,0,1:T(8,128)S(1)} %stack.161), channel_id=1, source_target_pairs={{8,0},{16,8},{24,16},{9,1},{17,9},{25,17},{10,2},{18,10},{26,18},{... | collective-permute-start | bytes 98312 | tf_op jit(solution)/shard_map/ppermute | solution.py:24
  10.9 0.8 copy-start.10
  12.3 67.3 %collective-permute-start.2 = (f32[18,1,8,128]{3,0,2,1:T(8,128)S(1)}, f32[18,1,8,128]{3,0,2,1:T(8,128)S(1)}, u32[]{:S(2)}, u32[]{:S(2)}) collective-permute-start(f32[18,1,8,128]{3,0,2,1:T(8,128)S(1)} %pad_maximum_fusion.4), channel_id=1, source_target_pairs={{0,1},{1,2},{2,3},{3,4},{4,5},{5,6},{6,7},{8,9},{9,10},{10,11},{11... | collective-permute-start | bytes 221192 | tf_op jit(solution)/shard_map/ppermute | solution.py:24
  15.7 63.9 %collective-permute-start.3 = (f32[18,1,8,128]{3,2,0,1:T(8,128)S(1)}, f32[18,1,8,128]{3,2,0,1:T(8,128)S(1)}, u32[]{:S(2)}, u32[]{:S(2)}) collective-permute-start(f32[18,1,8,128]{3,2,0,1:T(8,128)S(1)} %pad_maximum_fusion.5), channel_id=1, source_target_pairs={{1,0},{2,1},{3,2},{4,3},{5,4},{6,5},{7,6},{9,8},{10,9},{11,10},{12... | collective-permute-start | bytes 221192 | tf_op jit(solution)/shard_map/ppermute | solution.py:24
  18.3 0.7 copy-start.9
  80.7 0.7 copy-start.5
  80.7 0.7 copy-start.4
  100.0 0.8 copy-start.8
  100.0 7.3 %collective-permute-start.4 = (f32[8,128]{1,0:T(8,128)S(1)}, f32[8,128]{1,0:T(8,128)S(1)}, u32[]{:S(2)}, u32[]{:S(2)}) collective-permute-start(f32[8,128]{1,0:T(8,128)S(1)} %get-tuple-element.14), channel_id=1, source_target_pairs={{0,1},{1,0},{2,3},{3,2},{4,5},{5,4},{6,7},{7,6},{8,9},{9,8},{10,11... | collective-permute-start | bytes 12296 | tf_op jit(solution)/shard_map/ppermute | solution.py:36
  107.4 6.5 %collective-permute-start.5 = (f32[8,128]{1,0:T(8,128)S(1)}, f32[8,128]{1,0:T(8,128)S(1)}, u32[]{:S(2)}, u32[]{:S(2)}) collective-permute-start(f32[8,128]{1,0:T(8,128)S(1)} %max.15), channel_id=1, source_target_pairs={{0,2},{1,3},{2,0},{3,1},{4,6},{5,7},{6,4},{7,5},{8,10},{9,11},{10,... | collective-permute-start | bytes 12296 | tf_op jit(solution)/shard_map/ppermute | solution.py:36
  113.9 4.6 %collective-permute-start.6 = (f32[8,128]{1,0:T(8,128)S(1)}, f32[8,128]{1,0:T(8,128)S(1)}, u32[]{:S(2)}, u32[]{:S(2)}) collective-permute-start(f32[8,128]{1,0:T(8,128)S(1)} %max.16), channel_id=1, source_target_pairs={{0,4},{1,5},{2,6},{3,7},{4,0},{5,1},{6,2},{7,3},{8,12},{9,13},{10,... | collective-permute-start | bytes 12296 | tf_op jit(solution)/shard_map/ppermute | solution.py:36
  118.4 1.2 collective-permute-start.7
  119.6 12.9 %collective-permute-start.8 = (f32[8,128]{1,0:T(8,128)S(1)}, f32[8,128]{1,0:T(8,128)S(1)}, u32[]{:S(2)}, u32[]{:S(2)}) collective-permute-start(f32[8,128]{1,0:T(8,128)S(1)} %max.18), channel_id=1, source_target_pairs={{0,16},{8,24},{16,0},{24,8},{1,17},{9,25},{17,1},{25,9},{2,18},{10... | collective-permute-start | bytes 12296 | tf_op jit(solution)/shard_map/ppermute | solution.py:36
  121.0 14.4 %collective-permute-start.9 = (f32[9,14,128]{2,1,0:T(8,128)S(1)}, f32[9,14,128]{2,1,0:T(8,128)S(1)}, u32[]{:S(2)}, u32[]{:S(2)}) collective-permute-start(f32[9,14,128]{2,1,0:T(8,128)S(1)} %get-tuple-element.24), channel_id=1, source_target_pairs={{0,8},{8,16},{16,24},{1,9},{9,17},{17,25},{2,10},{10,18},{18,26},{... | collective-permute-start | bytes 193544 | tf_op jit(solution)/shard_map/ppermute | solution.py:24
  123.0 12.4 %collective-permute-start.10 = (f32[9,14,128]{2,1,0:T(8,128)S(1)}, f32[9,14,128]{2,1,0:T(8,128)S(1)}, u32[]{:S(2)}, u32[]{:S(2)}) collective-permute-start(f32[9,14,128]{2,1,0:T(8,128)S(1)} %get-tuple-element.25), channel_id=1, source_target_pairs={{8,0},{16,8},{24,16},{9,1},{17,9},{25,17},{10,2},{18,10},{26,18},{... | collective-permute-start | bytes 193544 | tf_op jit(solution)/shard_map/ppermute | solution.py:24
  126.6 8.8 %collective-permute-start.11 = (f32[9,14,128]{2,1,0:T(8,128)S(1)}, f32[9,14,128]{2,1,0:T(8,128)S(1)}, u32[]{:S(2)}, u32[]{:S(2)}) collective-permute-start(f32[9,14,128]{2,1,0:T(8,128)S(1)} %get-tuple-element.27), channel_id=1, source_target_pairs={{0,1},{1,2},{2,3},{3,4},{4,5},{5,6},{6,7},{8,9},{9,10},{10,11},{11... | collective-permute-start | bytes 193544 | tf_op jit(solution)/shard_map/ppermute | solution.py:24
  129.2 7.1 %collective-permute-start.12 = (f32[9,14,128]{2,1,0:T(8,128)S(1)}, f32[9,14,128]{2,1,0:T(8,128)S(1)}, u32[]{:S(2)}, u32[]{:S(2)}) collective-permute-start(f32[9,14,128]{2,1,0:T(8,128)S(1)} %get-tuple-element.26), channel_id=1, source_target_pairs={{1,0},{2,1},{3,2},{4,3},{5,4},{6,5},{7,6},{9,8},{10,9},{11,10},{12... | collective-permute-start | bytes 193544 | tf_op jit(solution)/shard_map/ppermute | solution.py:24

commit v4 on v3

--- a/solution.py
+++ b/solution.py
@@ -126,11 +126,19 @@
 
 
 def turn_columns(q_ref, columns_ref, blocks):
-    def turn(b, _):
-        columns_ref[b, :, 0:SUB] = jnp.transpose(q_ref[b])
-        return 0
-
-    lax.fori_loop(0, blocks, turn, 0, unroll=4)
+    lanes = q_ref.shape[2]
+    most = lanes // SUB
+    at_once = max(n for n in range(1, most + 1) if blocks % n == 0)
+
+    def turn(g, _):
+        rows = [q_ref[g * at_once + n] for n in range(at_once)]
+        rows += [jnp.zeros((SUB, lanes), f32)] * (most - at_once)
+        turned = jnp.transpose(jnp.concatenate(rows, axis=0))
+        for n in range(at_once):
+            columns_ref[g * at_once + n, :, 0:SUB] = turned[:, n * SUB : n * SUB + SUB]
+        return 0
+
+    lax.fori_loop(0, blocks // at_once, turn, 0)
 
 
 def own_kernel(
@@ -261,7 +269,7 @@
     highest, fastest = lax.fori_loop(0, blocks, close, (nothing, nothing), unroll=4)
     highest = jnp.max(highest, axis=1, keepdims=True)
     fastest = jnp.max(fastest, axis=1, keepdims=True)
-    first = lax.broadcasted_iota(jnp.int32, peak_ref.shape, 1) == 0
+    first = lax.broadcasted_iota(jnp.int32, peak_ref.shape, 0) == 0
     peak_ref[...] = jnp.where(first, highest, fastest)
 
 
@@ -457,7 +465,7 @@
         halo_count, halo, fields, own, windage.reshape(2, blocks, lanes), rows, cols
     )
     peaks = jnp.sqrt(everywhere_max(peak))
-    delta_t = time_step(peaks[0, 0], peaks[0, 1])
+    delta_t = time_step(peaks[0], peaks[1])
     moving = pick(slots, keep, late, ways)
     came = jnp.stack(send_on(jnp.concatenate([still, moving])))
 

time: 139 us -> 138 us (level)
    ppermute x8, waiting for transfers between devices: 0.95 us -> 3.19 us  [passed_along(): return lax.ppermute(array, axis, pairs)]
where the time goes in v4:
time: 138 us; the launch traced here: 137 us
  Pallas kernels  88.9 us (64%)
  starting transfers between devices  29.6 us (21%)
  local copies, waits for them, and re-layouts  7.99 us (6%)
  waiting for transfers between devices  5.99 us (4%)
  other arithmetic  2.63 us (2%)
    pallas_call x1, Pallas kernels, own_forces(): pl.pallas_call(functools.partial(own_kernel, rows=rows, cols=cols), out_s...  60.2 us
    ppermute x8, starting transfers between devices, passed_along(): return lax.ppermute(array, axis, pairs)  22.8 us
    pallas_call x1, Pallas kernels, halo_forces(): pl.pallas_call(halo_kernel, out_shape=(jax.ShapeDtypeStruct((3, blocks, l...  18.6 us
    pallas_call x2, Pallas kernels, pick(): pl.pallas_call(pick_kernel, out_shape=jax.ShapeDtypeStruct((count, rows,...  10.1 us
    ppermute x5, starting transfers between devices, everywhere_max(): array = jnp.maximum(array, lax.ppermute(array, axis, pairs))  6.8 us
    unnamed x43, local copies, waits for them, and re-layouts  5.36 us
    ppermute x8, waiting for transfers between devices, passed_along(): return lax.ppermute(array, axis, pairs)  3.19 us
    ppermute x5, waiting for transfers between devices, everywhere_max(): array = jnp.maximum(array, lax.ppermute(array, axis, pairs))  2.8 us
  transfers between devices with their start and end apart: 13, of which 3 were waited for; matrix products, arithmetic and copies ran while one was open for 2% of the time, Pallas kernels for 51%

profile of v4, /device:TPU:6, one launch (start us, length us, event | category | flops | bytes accessed | tf_op | source)
XLA Modules:
  0.0 136.8 jit_solution(2021161072012497321)
XLA Ops:
  0.7 0.8 copy.37
  1.5 0.9 fusion.37
  2.7 0.8 copy-done.3
  3.8 0.7 copy-done.7
  5.0 1.9 %collective-permute-start = (f32[1,8,8,128]{3,0,2,1:T(1,128)S(1)}, f32[1,8,8,128]{3,0,2,1:T(1,128)S(1)}, u32[]{:S(2)}, u32[]{:S(2)}) collective-permute-start(f32[1,8,8,128]{3,0,2,1:T(1,128)S(1)} %constant_dynamic-update-slice_fusion), channel_id=1, source_target_pairs={{0,8},{8,16},{16,24},{1,9},{9,17},{17,25},{2,10},{10,18},{18,26},{... | collective-permute-start | bytes 98312 | tf_op jit(solution)/shard_map/ppermute | solution.py:24
  7.0 3.6 %collective-permute-start.1 = (f32[1,8,8,128]{3,2,0,1:T(8,128)S(1)}, f32[1,8,8,128]{3,2,0,1:T(8,128)S(1)}, u32[]{:S(2)}, u32[]{:S(2)}) collective-permute-start(f32[1,8,8,128]{3,2,0,1:T(8,128)S(1)} %stack.161), channel_id=1, source_target_pairs={{8,0},{16,8},{24,16},{9,1},{17,9},{25,17},{10,2},{18,10},{26,18},{... | collective-permute-start | bytes 98312 | tf_op jit(solution)/shard_map/ppermute | solution.py:24
  12.3 3.4 %collective-permute-start.2 = (f32[18,1,8,128]{3,0,2,1:T(8,128)S(1)}, f32[18,1,8,128]{3,0,2,1:T(8,128)S(1)}, u32[]{:S(2)}, u32[]{:S(2)}) collective-permute-start(f32[18,1,8,128]{3,0,2,1:T(8,128)S(1)} %pad_maximum_fusion.4), channel_id=1, source_target_pairs={{0,1},{1,2},{2,3},{3,4},{4,5},{5,6},{6,7},{8,9},{9,10},{10,11},{11... | collective-permute-start | bytes 221192 | tf_op jit(solution)/shard_map/ppermute | solution.py:24
  15.7 2.4 %collective-permute-start.3 = (f32[18,1,8,128]{3,2,0,1:T(8,128)S(1)}, f32[18,1,8,128]{3,2,0,1:T(8,128)S(1)}, u32[]{:S(2)}, u32[]{:S(2)}) collective-permute-start(f32[18,1,8,128]{3,2,0,1:T(8,128)S(1)} %pad_maximum_fusion.5), channel_id=1, source_target_pairs={{1,0},{2,1},{3,2},{4,3},{5,4},{6,5},{7,6},{9,8},{10,9},{11,10},{12... | collective-permute-start | bytes 221192 | tf_op jit(solution)/shard_map/ppermute | solution.py:24
  19.1 60.2 %shard_map.122 = (f32[128,8,128]{2,1,0:T(8,128)S(1)}, f32[128,8,128]{2,1,0:T(8,128)S(1)}) custom-call(s32[128]{0:T(128)S(1)} %reshape.128.count_ref, f32[2,128,128]{2,1,0:T(8,128)S(1)} %bitcast.150, f32[2,128,128]{2,1,0:T(8,128)S(1)} %bitcast.151, f32[128,128]{1,0:T(8,128)S(1)} %bitcast.153, f32[128,128]{1,0:T(8,128)S(1)} %bitcast.154), custom_call_target="tpu_custom_call" | custom-call | flops 400000000 | bytes 2000000 | tf_op jit(solution)/shard_map/pallas_call | solution.py:304
  79.4 1.0 fusion.12.count_ref
  81.1 18.6 %shard_map.123 = (f32[3,128,128]{2,1,0:T(8,128)S(1)}, f32[8,128]{1,0:T(8,128)S(1)}) custom-call(s32[52]{0:T(128)S(1)} %fusion.12.count_ref, s32[312]{0:T(512)S(1)} %copy-done.4, f32[312]{0:T(512)S(1)} %copy-done.5, f32[52,8,128]{2,1,0:T(8,128)S(1)} %pad_maximum_fusion.3.halo_ref, f32[128,8,128]{2,1,0:T(8,128)S(1)} %get-tuple-element.12.q_ref, ...), custom_call_target="tpu_custom_call" | custom-call | tf_op jit(solution)/shard_map/pallas_call | solution.py:323
  100.5 6.5 %shard_map.124 = f32[6,56,128]{2,1,0:T(8,128)S(1)} custom-call(s32[56,128]{1,0:T(8,128)S(1)} %reshape.135.slot_ref, f32[56,128]{1,0:T(8,128)S(1)} %compare_convert_fusion.keep_ref, f32[6,128,128]{2,1,0:T(8,128)S(1)} %get-tuple-element.20.table_ref), custom_call_target="tpu_custom_call" | custom-call | tf_op jit(solution)/shard_map/pallas_call | solution.py:373
  107.0 2.3 %collective-permute-start.5 = (f32[8,128]{1,0:T(8,128)S(1)}, f32[8,128]{1,0:T(8,128)S(1)}, u32[]{:S(2)}, u32[]{:S(2)}) collective-permute-start(f32[8,128]{1,0:T(8,128)S(1)} %max.15), channel_id=1, source_target_pairs={{0,2},{1,3},{2,0},{3,1},{4,6},{5,7},{6,4},{7,5},{8,10},{9,11},{10,... | collective-permute-start | bytes 12296 | tf_op jit(solution)/shard_map/ppermute | solution.py:36
  109.4 3.6 %shard_map.125 = f32[3,56,128]{2,1,0:T(8,128)S(1)} custom-call(s32[56,128]{1,0:T(8,128)S(1)} %reshape.135.slot_ref, f32[56,128]{1,0:T(8,128)S(1)} %compare_convert_fusion.keep_ref, f32[3,128,128]{2,1,0:T(8,128)S(1)} %get-tuple-element.15.table_ref), custom_call_target="tpu_custom_call" | custom-call | tf_op jit(solution)/shard_map/pallas_call | solution.py:373
  113.0 2.9 %collective-permute-start.6 = (f32[8,128]{1,0:T(8,128)S(1)}, f32[8,128]{1,0:T(8,128)S(1)}, u32[]{:S(2)}, u32[]{:S(2)}) collective-permute-start(f32[8,128]{1,0:T(8,128)S(1)} %max.16), channel_id=1, source_target_pairs={{0,4},{1,5},{2,6},{3,7},{4,0},{5,1},{6,2},{7,3},{8,12},{9,13},{10,... | collective-permute-start | bytes 12296 | tf_op jit(solution)/shard_map/ppermute | solution.py:36
  116.0 1.6 %collective-permute-done.6 = f32[8,128]{1,0:T(8,128)S(1)} collective-permute-done((f32[8,128]{1,0:T(8,128)S(1)}, f32[8,128]{1,0:T(8,128)S(1)}, u32[]{:S(2)}, u32[]{:S(2)}) %collective-permute-start.6) | collective-permute-done | bytes 4128 | tf_op jit(solution)/shard_map/ppermute | solution.py:36
  117.6 1.1 collective-permute-done.7
  118.8 1.6 %collective-permute-start.8 = (f32[8,128]{1,0:T(8,128)S(1)}, f32[8,128]{1,0:T(8,128)S(1)}, u32[]{:S(2)}, u32[]{:S(2)}) collective-permute-start(f32[8,128]{1,0:T(8,128)S(1)} %max.18), channel_id=1, source_target_pairs={{0,16},{8,24},{16,0},{24,8},{1,17},{9,25},{17,1},{25,9},{2,18},{10... | collective-permute-start | bytes 12296 | tf_op jit(solution)/shard_map/ppermute | solution.py:36
  120.3 2.0 %collective-permute-start.9 = (f32[9,14,128]{2,1,0:T(8,128)S(1)}, f32[9,14,128]{2,1,0:T(8,128)S(1)}, u32[]{:S(2)}, u32[]{:S(2)}) collective-permute-start(f32[9,14,128]{2,1,0:T(8,128)S(1)} %get-tuple-element.24), channel_id=1, source_target_pairs={{0,8},{8,16},{16,24},{1,9},{9,17},{17,25},{2,10},{10,18},{18,26},{... | collective-permute-start | bytes 193544 | tf_op jit(solution)/shard_map/ppermute | solution.py:24
  122.3 3.6 %collective-permute-start.10 = (f32[9,14,128]{2,1,0:T(8,128)S(1)}, f32[9,14,128]{2,1,0:T(8,128)S(1)}, u32[]{:S(2)}, u32[]{:S(2)}) collective-permute-start(f32[9,14,128]{2,1,0:T(8,128)S(1)} %get-tuple-element.25), channel_id=1, source_target_pairs={{8,0},{16,8},{24,16},{9,1},{17,9},{25,17},{10,2},{18,10},{26,18},{... | collective-permute-start | bytes 193544 | tf_op jit(solution)/shard_map/ppermute | solution.py:24
  125.9 2.9 %collective-permute-start.11 = (f32[9,14,128]{2,1,0:T(8,128)S(1)}, f32[9,14,128]{2,1,0:T(8,128)S(1)}, u32[]{:S(2)}, u32[]{:S(2)}) collective-permute-start(f32[9,14,128]{2,1,0:T(8,128)S(1)} %get-tuple-element.27), channel_id=1, source_target_pairs={{0,1},{1,2},{2,3},{3,4},{4,5},{5,6},{6,7},{8,9},{9,10},{10,11},{11... | collective-permute-start | bytes 193544 | tf_op jit(solution)/shard_map/ppermute | solution.py:24
  128.8 3.0 %collective-permute-start.12 = (f32[9,14,128]{2,1,0:T(8,128)S(1)}, f32[9,14,128]{2,1,0:T(8,128)S(1)}, u32[]{:S(2)}, u32[]{:S(2)}) collective-permute-start(f32[9,14,128]{2,1,0:T(8,128)S(1)} %get-tuple-element.26), channel_id=1, source_target_pairs={{1,0},{2,1},{3,2},{4,3},{5,4},{6,5},{7,6},{9,8},{10,9},{11,10},{12... | collective-permute-start | bytes 193544 | tf_op jit(solution)/shard_map/ppermute | solution.py:24
  132.0 0.8 pad_maximum_fusion
  132.8 3.2 %collective-permute-done.12 = f32[9,14,128]{2,1,0:T(8,128)S(1)} collective-permute-done((f32[9,14,128]{2,1,0:T(8,128)S(1)}, f32[9,14,128]{2,1,0:T(8,128)S(1)}, u32[]{:S(2)}, u32[]{:S(2)}) %collective-permute-start.12) | collective-permute-done | bytes 64544 | tf_op jit(solution)/shard_map/ppermute | solution.py:24
  (110 shorter events, 6.0 us)
Async XLA Ops:
  0.6 10.4 %copy-start = (f32[2,16]{1,0:T(2,128)S(1)}, f32[2,16]{1,0:T(2,128)}, u32[]{:S(2)}) copy-start(f32[2,16]{1,0:T(2,128)} %param.17) | copy-start | bytes 388
  0.6 0.8 copy-start.6
  1.5 1.0 copy-start.1
  1.5 1.0 copy-start.2
  2.6 0.8 copy-start.3
  3.7 0.8 copy-start.7
  5.0 7.3 %collective-permute-start = (f32[1,8,8,128]{3,0,2,1:T(1,128)S(1)}, f32[1,8,8,128]{3,0,2,1:T(1,128)S(1)}, u32[]{:S(2)}, u32[]{:S(2)}) collective-permute-start(f32[1,8,8,128]{3,0,2,1:T(1,128)S(1)} %constant_dynamic-update-slice_fusion), channel_id=1, source_target_pairs={{0,8},{8,16},{16,24},{1,9},{9,17},{17,25},{2,10},{10,18},{18,26},{... | collective-permute-start | bytes 98312 | tf_op jit(solution)/shard_map/ppermute | solution.py:24
  7.0 5.2 %collective-permute-start.1 = (f32[1,8,8,128]{3,2,0,1:T(8,128)S(1)}, f32[1,8,8,128]{3,2,0,1:T(8,128)S(1)}, u32[]{:S(2)}, u32[]{:S(2)}) collective-permute-start(f32[1,8,8,128]{3,2,0,1:T(8,128)S(1)} %stack.161), channel_id=1, source_target_pairs={{8,0},{16,8},{24,16},{9,1},{17,9},{25,17},{10,2},{18,10},{26,18},{... | collective-permute-start | bytes 98312 | tf_op jit(solution)/shard_map/ppermute | solution.py:24
  10.9 0.8 copy-start.10
  12.3 67.0 %collective-permute-start.2 = (f32[18,1,8,128]{3,0,2,1:T(8,128)S(1)}, f32[18,1,8,128]{3,0,2,1:T(8,128)S(1)}, u32[]{:S(2)}, u32[]{:S(2)}) collective-permute-start(f32[18,1,8,128]{3,0,2,1:T(8,128)S(1)} %pad_maximum_fusion.4), channel_id=1, source_target_pairs={{0,1},{1,2},{2,3},{3,4},{4,5},{5,6},{6,7},{8,9},{9,10},{10,11},{11... | collective-permute-start | bytes 221192 | tf_op jit(solution)/shard_map/ppermute | solution.py:24
  15.7 63.6 %collective-permute-start.3 = (f32[18,1,8,128]{3,2,0,1:T(8,128)S(1)}, f32[18,1,8,128]{3,2,0,1:T(8,128)S(1)}, u32[]{:S(2)}, u32[]{:S(2)}) collective-permute-start(f32[18,1,8,128]{3,2,0,1:T(8,128)S(1)} %pad_maximum_fusion.5), channel_id=1, source_target_pairs={{1,0},{2,1},{3,2},{4,3},{5,4},{6,5},{7,6},{9,8},{10,9},{11,10},{12... | collective-permute-start | bytes 221192 | tf_op jit(solution)/shard_map/ppermute | solution.py:24
  18.3 0.7 copy-start.9
  80.4 0.7 copy-start.5
  80.4 0.7 copy-start.4
  99.7 0.8 copy-start.8
  99.7 7.3 %collective-permute-start.4 = (f32[8,128]{1,0:T(8,128)S(1)}, f32[8,128]{1,0:T(8,128)S(1)}, u32[]{:S(2)}, u32[]{:S(2)}) collective-permute-start(f32[8,128]{1,0:T(8,128)S(1)} %get-tuple-element.14), channel_id=1, source_target_pairs={{0,1},{1,0},{2,3},{3,2},{4,5},{5,4},{6,7},{7,6},{8,9},{9,8},{10,11... | collective-permute-start | bytes 12296 | tf_op jit(solution)/shard_map/ppermute | solution.py:36
  107.0 6.0 %collective-permute-start.5 = (f32[8,128]{1,0:T(8,128)S(1)}, f32[8,128]{1,0:T(8,128)S(1)}, u32[]{:S(2)}, u32[]{:S(2)}) collective-permute-start(f32[8,128]{1,0:T(8,128)S(1)} %max.15), channel_id=1, source_target_pairs={{0,2},{1,3},{2,0},{3,1},{4,6},{5,7},{6,4},{7,5},{8,10},{9,11},{10,... | collective-permute-start | bytes 12296 | tf_op jit(solution)/shard_map/ppermute | solution.py:36
  113.0 4.6 %collective-permute-start.6 = (f32[8,128]{1,0:T(8,128)S(1)}, f32[8,128]{1,0:T(8,128)S(1)}, u32[]{:S(2)}, u32[]{:S(2)}) collective-permute-start(f32[8,128]{1,0:T(8,128)S(1)} %max.16), channel_id=1, source_target_pairs={{0,4},{1,5},{2,6},{3,7},{4,0},{5,1},{6,2},{7,3},{8,12},{9,13},{10,... | collective-permute-start | bytes 12296 | tf_op jit(solution)/shard_map/ppermute | solution.py:36
  117.6 1.2 collective-permute-start.7
  118.8 13.0 %collective-permute-start.8 = (f32[8,128]{1,0:T(8,128)S(1)}, f32[8,128]{1,0:T(8,128)S(1)}, u32[]{:S(2)}, u32[]{:S(2)}) collective-permute-start(f32[8,128]{1,0:T(8,128)S(1)} %max.18), channel_id=1, source_target_pairs={{0,16},{8,24},{16,0},{24,8},{1,17},{9,25},{17,1},{25,9},{2,18},{10... | collective-permute-start | bytes 12296 | tf_op jit(solution)/shard_map/ppermute | solution.py:36
  120.3 12.4 %collective-permute-start.9 = (f32[9,14,128]{2,1,0:T(8,128)S(1)}, f32[9,14,128]{2,1,0:T(8,128)S(1)}, u32[]{:S(2)}, u32[]{:S(2)}) collective-permute-start(f32[9,14,128]{2,1,0:T(8,128)S(1)} %get-tuple-element.24), channel_id=1, source_target_pairs={{0,8},{8,16},{16,24},{1,9},{9,17},{17,25},{2,10},{10,18},{18,26},{... | collective-permute-start | bytes 193544 | tf_op jit(solution)/shard_map/ppermute | solution.py:24
  122.3 10.4 %collective-permute-start.10 = (f32[9,14,128]{2,1,0:T(8,128)S(1)}, f32[9,14,128]{2,1,0:T(8,128)S(1)}, u32[]{:S(2)}, u32[]{:S(2)}) collective-permute-start(f32[9,14,128]{2,1,0:T(8,128)S(1)} %get-tuple-element.25), channel_id=1, source_target_pairs={{8,0},{16,8},{24,16},{9,1},{17,9},{25,17},{10,2},{18,10},{26,18},{... | collective-permute-start | bytes 193544 | tf_op jit(solution)/shard_map/ppermute | solution.py:24
  125.9 6.9 %collective-permute-start.11 = (f32[9,14,128]{2,1,0:T(8,128)S(1)}, f32[9,14,128]{2,1,0:T(8,128)S(1)}, u32[]{:S(2)}, u32[]{:S(2)}) collective-permute-start(f32[9,14,128]{2,1,0:T(8,128)S(1)} %get-tuple-element.27), channel_id=1, source_target_pairs={{0,1},{1,2},{2,3},{3,4},{4,5},{5,6},{6,7},{8,9},{9,10},{10,11},{11... | collective-permute-start | bytes 193544 | tf_op jit(solution)/shard_map/ppermute | solution.py:24
  128.8 7.1 %collective-permute-start.12 = (f32[9,14,128]{2,1,0:T(8,128)S(1)}, f32[9,14,128]{2,1,0:T(8,128)S(1)}, u32[]{:S(2)}, u32[]{:S(2)}) collective-permute-start(f32[9,14,128]{2,1,0:T(8,128)S(1)} %get-tuple-element.26), channel_id=1, source_target_pairs={{1,0},{2,1},{3,2},{4,3},{5,4},{6,5},{7,6},{9,8},{10,9},{11,10},{12... | collective-permute-start | bytes 193544 | tf_op jit(solution)/shard_map/ppermute | solution.py:24
